TPU v7x, 32 devices: a whole 2x2x4 slice. The times are simulated.
32 devices in a mesh: parts: 2 (over y), rep: 4 (over x, core), tp: 4 (over z).
Axes of the slice: x: 2, y: 2, z: 4, core: 2. Of those that a mesh axis runs over, the one named last changes fastest.
Arguments:
- queries: bfloat16 [512, 4, 4096], P(('parts', 'rep', 'tp')), parts along dimension 0, may hold values from -16 to 16
- cached_key_store: bfloat16 [512, 4, 128, 128], P(('parts', 'rep', 'tp')), parts along dimension 0, may hold values from -6 to 6
- cached_value_store: bfloat16 [512, 4, 128, 128], P(('parts', 'rep', 'tp')), parts along dimension 0, may hold values from -6 to 6
- decode_step_keys: bfloat16 [512, 4, 4, 128], P(('parts', 'rep', 'tp')), parts along dimension 0, may hold values from -6 to 6
- decode_step_values: bfloat16 [512, 4, 4, 128], P(('parts', 'rep', 'tp')), parts along dimension 0, may hold values from -6 to 6
- request_cache_length: int32 [512], P(('parts', 'rep', 'tp')), parts along dimension 0, may hold values from 2 to 128, as said below
- output_projection_weight: bfloat16 [4096, 4096], P('tp'), may hold values from -0.09375 to 0.09375
- adapter_down_weight: bfloat16 [8, 4096, 128], P('rep', 'tp'), may hold values from -0.09375 to 0.09375
- adapter_up_weight: bfloat16 [8, 128, 4096], P('rep', None, 'tp'), may hold values from -0.5 to 0.5
- adapter_store_slot: int32 [8], replicated, may hold values from 0 to 7, as said below
- adapter_ranks: int32 [8], replicated, may hold values from 8 to 128, as said below
- request_block_adapter: int32 [16], P('rep'), may hold values from 0 to 7, as said below
Outputs:
- attn_proj: bfloat16 [512, 4, 4096], P(('parts', 'rep'), None, 'tp'), parts along dimension 0
There are 2 independent parts, one for each index of `parts`. A program takes and returns all parts, laid end to end along the dimension named above; an argument that names none is the same for every part. Nothing has to cross between parts.
Inputs may be any that keep to these rules, and one draw needn't show every extreme that they name: `request_cache_length`: some request has exactly 128 live positions. A permutation; adapter a lives at index adapter_store_slot[a] of adapter_down_weight and adapter_up_weight, on replica adapter_store_slot[a] // 2. `adapter_ranks`: 128 divided by a power of two; both ends occur. `request_block_adapter`: the 4 blocks of one replica use adapters that live on 4 different replicas; one replica holds an adapter of a block from every replica.
All inputs are finite; a program needn't handle non-finite values.
Results may differ from a plain program's by a relative error of at most 0.012.
Values may be sent and summed in bfloat16 or wider, within the bound.
No kernel may reach another device: no remote copies, remote signals or barrier semaphores. Data moves between devices by JAX's collectives and lax.ppermute only.
A program may use at most 64 MiB of HBM per device.

v0:
```python
import functools
import math

import jax
import jax.numpy as jnp
from jax import lax
from jax.experimental import pallas as pl
from jax.experimental.pallas import tpu as pltpu
from jax.sharding import PartitionSpec as P

adapter_alpha = 16.0
lanes = 128
f32 = jnp.float32
bf16 = jnp.bfloat16
hint = pl.CostEstimate(flops=1, bytes_accessed=1, transcendentals=0)


def swap(x, axis, bit):
    n = lax.axis_size(axis)
    return lax.ppermute(x, axis, [(i, i ^ bit) for i in range(n)])


def in_hbm(x):
    return pltpu.with_memory_space_constraint(x, pltpu.HBM)


def in_vmem(x):
    return pltpu.with_memory_space_constraint(x, pltpu.VMEM)


def attend_kernel(me_ref, len_ref, q_ref, dk_ref, dv_ref, *refs, pieces, n_tp, kv_count):
    count = len(pieces)
    k_refs, v_refs, outs = refs[:count], refs[count : 2 * count], refs[-count:]
    reqs, steps, width = q_ref.shape
    cache_len, head = k_refs[0].shape[2:]
    heads_each = width // head // n_tp
    group = width // head // kv_count
    feats = heads_each * head
    rows = heads_each * steps
    me = me_ref[0]
    scale = math.log2(math.e) / math.sqrt(head)
    fresh = steps * kv_count
    shape = (count * rows, lanes)
    row = lax.broadcasted_iota(jnp.int32, shape, 0)
    col = lax.broadcasted_iota(jnp.int32, shape, 1)
    row_kv = jnp.zeros(shape, jnp.int32)
    for u, p in enumerate(pieces):
        row_kv = jnp.where(row // rows == u, (me ^ p) * heads_each // group, row_kv)
    visible = (col % kv_count == row_kv) & (col // kv_count <= row % steps) & (col < fresh)
    base = pl.program_id(0) * reqs
    contract = (((1,), (1,)), ((), ()))
    pad = jnp.zeros((lanes - fresh, head), f32)

    def steps_of(ref, r):
        return jnp.concatenate([ref[r, t].astype(f32) for t in range(steps)] + [pad], axis=0).astype(bf16)

    old, new = [], []
    for r in range(reqs):
        parts = []
        for p in pieces:
            for g in range(heads_each):
                at = pl.multiple_of((me ^ p) * feats + g * head, lanes)
                parts.append(q_ref[r, :, pl.ds(at, head)].astype(f32))
        query = jnp.concatenate(parts, axis=0).astype(bf16)
        old.append(
            jnp.concatenate(
                [
                    lax.dot_general(
                        query[u * rows : (u + 1) * rows], k_refs[u][r, 0], contract, preferred_element_type=f32
                    )
                    for u in range(count)
                ],
                axis=0,
            )
        )
        new.append(lax.dot_general(query, steps_of(dk_ref, r), contract, preferred_element_type=f32))
    share, old_weight, new_weight = [], [], []
    for r in range(reqs):
        a = jnp.where(col < len_ref[base + r], old[r], -jnp.inf)
        b = jnp.where(visible, new[r], -jnp.inf)
        top = jnp.max(jnp.maximum(a, b), -1, keepdims=True)
        a = jnp.exp2((a - top) * scale)
        b = jnp.exp2((b - top) * scale)
        share.append(1.0 / jnp.sum(a + b, -1, keepdims=True))
        old_weight.append(a.astype(bf16))
        new_weight.append(b.astype(bf16))
    mixed = []
    for r in range(reqs):
        o = jnp.concatenate(
            [
                jnp.dot(old_weight[r][u * rows : (u + 1) * rows], v_refs[u][r, 0], preferred_element_type=f32)
                for u in range(count)
            ],
            axis=0,
        )
        o += jnp.dot(new_weight[r], steps_of(dv_ref, r), preferred_element_type=f32)
        mixed.append(o * share[r])
    for u in range(count):
        for g in range(heads_each):
            at = u * rows + g * steps
            stacked = jnp.concatenate([o[at : at + steps] for o in mixed], axis=0)
            outs[u][:, g * head : (g + 1) * head] = stacked.astype(bf16)


def attend(q, keys, values, new_keys, new_values, lengths, me, pieces, n_tp, waits=()):
    count, steps, width = q.shape
    kv_count, cache_len, head = keys.shape[1:]
    heads_each = width // head // n_tp
    group = width // head // kv_count
    assert group % heads_each == 0
    reqs = min(count, 8)
    feats = width // n_tp

    def cache_spec(p):
        return pl.BlockSpec(
            (reqs, 1, cache_len, head), lambda i, me, *_: (i, (me[0] ^ p) * heads_each // group, 0, 0)
        )

    q, keys, values, new_keys, new_values, lengths = map(
        in_hbm, (q, keys, values, new_keys, new_values, lengths)
    )
    return pl.pallas_call(
        functools.partial(attend_kernel, pieces=pieces, n_tp=n_tp, kv_count=kv_count),
        grid_spec=pltpu.PrefetchScalarGridSpec(
            num_scalar_prefetch=2,
            grid=(count // reqs,),
            in_specs=[
                pl.BlockSpec((reqs, steps, width), lambda i, *_: (i, 0, 0)),
                pl.BlockSpec((reqs, steps, kv_count, head), lambda i, *_: (i, 0, 0, 0)),
                pl.BlockSpec((reqs, steps, kv_count, head), lambda i, *_: (i, 0, 0, 0)),
            ]
            + [cache_spec(p) for p in pieces] * 2
            + [pl.BlockSpec(memory_space=pl.ANY)] * len(waits),
            out_specs=[pl.BlockSpec((reqs * steps, feats), lambda i, *_: (i, 0))] * len(pieces),
        ),
        out_shape=[jax.ShapeDtypeStruct((count * steps, feats), bf16)] * len(pieces),
        compiler_params=pltpu.CompilerParams(vmem_limit_bytes=32 << 20),
        cost_estimate=hint,
        name="attention",
    )(me, lengths, q, new_keys, new_values, *([keys] * len(pieces)), *([values] * len(pieces)), *waits)


def weight_copies(me, w_ref, out, sems, owners, columns, start, width):
    copies = []
    for u, p in enumerate(owners):
        at = pl.multiple_of((me ^ p) * columns + start, lanes)
        copies.append(
            pltpu.make_async_copy(
                w_ref.at[:, pl.ds(at, width)], out.at[:, u * width : (u + 1) * width], sems.at[u]
            )
        )
    return copies


def load_kernel(me_ref, w_ref, *refs, owners, part, columns):
    out_ref, sems = refs[-2:]
    copies = weight_copies(me_ref[0], w_ref, out_ref, sems, owners, columns, 0, part)
    for copy in copies:
        copy.start()
    for copy in copies:
        copy.wait()


def load(weight, me, owners, part, columns, waits):
    return pl.pallas_call(
        functools.partial(load_kernel, owners=owners, part=part, columns=columns),
        in_specs=[pl.BlockSpec(memory_space=pltpu.SMEM)]
        + [pl.BlockSpec(memory_space=pl.ANY)] * (1 + len(waits)),
        out_specs=pl.BlockSpec(memory_space=pltpu.VMEM),
        out_shape=pltpu.VMEM((weight.shape[0], len(owners) * part), weight.dtype),
        scratch_shapes=[pltpu.SemaphoreType.DMA((len(owners),))],
        compiler_params=pltpu.CompilerParams(vmem_limit_bytes=8 << 20),
        cost_estimate=hint,
        name="load",
    )(me, in_hbm(weight), *waits)


def block_place(table, b):
    rep_ref, adapter_ref, slot_ref, rank_ref, held = table
    adapter = adapter_ref[b]
    slot = slot_ref[adapter]
    return (slot // held) ^ rep_ref[0], slot % held, rank_ref[adapter]


def project_kernel(me_ref, *refs):
    *pieces, w_ref, out_ref, x_ref = refs
    rows = pieces[0].shape[0]
    for p, piece in enumerate(pieces):
        x_ref[pl.ds(pl.multiple_of((me_ref[0] ^ p) * rows, rows), rows), :] = piece[...]
    out_ref[...] = jnp.dot(x_ref[...], w_ref[...], preferred_element_type=f32).astype(bf16)


def project(pieces, weight, me):
    total = sum(x.shape[0] for x in pieces)
    return pl.pallas_call(
        project_kernel,
        in_specs=[pl.BlockSpec(memory_space=pltpu.SMEM)]
        + [pl.BlockSpec(memory_space=pltpu.VMEM)] * (len(pieces) + 1),
        out_specs=[pl.BlockSpec(memory_space=pltpu.VMEM)] * 2,
        out_shape=[
            jax.ShapeDtypeStruct((total, weight.shape[1]), bf16),
            jax.ShapeDtypeStruct((total, pieces[0].shape[1]), bf16),
        ],
        compiler_params=pltpu.CompilerParams(vmem_limit_bytes=8 << 20),
        cost_estimate=hint,
        name="projection",
    )(me, *pieces, in_vmem(weight))


def project_rest_kernel(me_ref, *refs, order, widths, columns, adapters, per_block, held):
    table, refs = (*refs[:4], held), refs[4:]
    x_ref, w_ref, downs, refs = refs[0], refs[1], refs[2 : 2 + adapters], refs[2 + adapters :]
    parts, owners = len(widths), len(order) // 2
    outs, keep_ref, low_ref = refs[: parts - 1], refs[parts - 1], refs[parts]
    nears, sems = refs[parts + 1 : -1], refs[-1]
    starts = [sum(widths[:q]) for q in range(parts)]
    jobs = [(order[:owners], q) for q in range(1, parts)] + [(order[owners:], q) for q in range(parts)]
    copies = [
        weight_copies(me_ref[0], w_ref, near, sems.at[h], relative, columns, starts[q], widths[q])
        for h, (near, (relative, q)) in enumerate(zip(nears, jobs))
    ]
    for group in copies:
        for copy in group:
            copy.start()
    for start in range(0, x_ref.shape[0], per_block):
        home, place, _ = block_place(table, start // per_block)
        here = slice(start, start + per_block)
        for i in range(adapters):

            @pl.when(home == i)
            def _():
                got = jnp.dot(x_ref[here, :], downs[i][place], preferred_element_type=f32)
                low_ref[here, :] = got
                outs[0][here, owners * widths[1] :] = got.astype(bf16)

    for h, (near, (_, q)) in enumerate(zip(nears, jobs)):
        for copy in copies[h]:
            copy.wait()
        got = jnp.dot(x_ref[...], near[...], preferred_element_type=f32).astype(bf16)
        wide = owners * widths[q]
        if h < parts - 1:
            outs[h][:, :wide] = got
        else:
            keep_ref[:, owners * starts[q] : owners * starts[q] + wide] = got


def project_rest(x, weight, downs, me, table, order, widths, columns, per_block):
    rows, feats = x.shape
    parts, owners = len(widths), len(order) // 2
    held, _, rank = downs[0].shape
    shapes = [(rows, owners * w) for w in (*widths[1:], columns)]
    shapes[0] = (rows, owners * widths[1] + rank)
    vmem = pl.BlockSpec(memory_space=pltpu.VMEM)
    return pl.pallas_call(
        functools.partial(
            project_rest_kernel,
            order=order,
            widths=widths,
            columns=columns,
            adapters=len(downs),
            per_block=per_block,
            held=held,
        ),
        in_specs=[pl.BlockSpec(memory_space=pltpu.SMEM)] * (1 + len(table))
        + [vmem, pl.BlockSpec(memory_space=pl.ANY)]
        + [vmem] * len(downs),
        out_specs=[vmem] * (parts + 1),
        out_shape=[jax.ShapeDtypeStruct(shape, bf16) for shape in shapes]
        + [jax.ShapeDtypeStruct((rows, rank), f32)],
        scratch_shapes=[pltpu.VMEM((feats, owners * w), weight.dtype) for w in (*widths[1:], *widths)]
        + [pltpu.SemaphoreType.DMA((2 * parts - 1, owners))],
        compiler_params=pltpu.CompilerParams(vmem_limit_bytes=20 << 20),
        cost_estimate=hint,
        name="projection_rest",
    )(me, *map(in_hbm, table), x, in_hbm(weight), *downs)


def combine_kernel(*refs, offsets, wide, with_low, waits):
    refs = refs[waits:]
    n = len(offsets)
    addends, refs = refs[:n], refs[n:]
    total = sum(a[:, off : off + wide].astype(f32) for a, off in zip(addends, offsets))
    if with_low:
        low_ref, send_ref, low_out_ref = refs
        low = low_ref[...] + addends[-1][:, addends[-1].shape[1] - lanes :].astype(f32)
        low_out_ref[...] = low
        send_ref[:, wide:] = low.astype(bf16)
    else:
        (send_ref,) = refs
    send_ref[:, :wide] = total.astype(bf16)


def combine(addends, wide, low, waits):
    arrays = [a for a, _ in addends]
    rows = arrays[0].shape[0]
    rank = 0 if low is None else low.shape[1]
    out_shape = [jax.ShapeDtypeStruct((rows, wide + rank), bf16)]
    if low is not None:
        arrays.append(low)
        out_shape.append(jax.ShapeDtypeStruct((rows, rank), f32))
    return pl.pallas_call(
        functools.partial(
            combine_kernel,
            offsets=[off for _, off in addends],
            wide=wide,
            with_low=low is not None,
            waits=len(waits),
        ),
        in_specs=[pl.BlockSpec(memory_space=pl.ANY)] * len(waits)
        + [pl.BlockSpec(memory_space=pltpu.VMEM)] * len(arrays),
        out_specs=[pl.BlockSpec(memory_space=pltpu.VMEM)] * len(out_shape),
        out_shape=out_shape,
        compiler_params=pltpu.CompilerParams(vmem_limit_bytes=8 << 20),
        cost_estimate=hint,
        name="combine",
    )(*waits, *arrays)


def finish_kernel(*refs, offsets, widths, first, n_rep, per_block, held):
    table, refs = (*refs[:4], held), refs[4:]
    addends = []
    for part_offsets in offsets:
        addends.append(list(zip(refs, part_offsets)))
        refs = refs[len(part_offsets) :]
    low_ref, got_ref, refs = refs[0], refs[1], refs[2:]
    ups, refs = refs[:n_rep], refs[n_rep:]
    out_ref, delta_ref, done_ref, sem = refs[-4:]
    steps = out_ref.shape[1]
    total_rows, rank_most = low_ref.shape
    low = low_ref[...] + got_ref[:, got_ref.shape[1] - rank_most :].astype(f32)
    column = lax.broadcasted_iota(jnp.int32, (per_block, rank_most), 1)
    here_columns = slice(first, first + sum(widths))
    for start in range(0, total_rows, per_block):
        home, place, rank = block_place(table, start // per_block)
        here = slice(start, start + per_block)
        factor = adapter_alpha / rank.astype(f32)
        scaled = jnp.where(column < rank, low[here] * factor, 0.0).astype(bf16)
        for i in range(n_rep):

            @pl.when(home == i)
            def _():
                delta_ref[here, :] = jnp.dot(
                    scaled, ups[i][place, :, here_columns], preferred_element_type=f32
                )

    for start in range(0, total_rows, per_block):
        here = slice(start, start + per_block)
        at = 0
        for pairs, width in zip(addends, widths):
            there = slice(at, at + width)
            total = sum(a[here, off : off + width].astype(f32) for a, off in pairs)
            total += delta_ref[here, there].astype(bf16).astype(f32)
            for r in range(per_block // steps):
                done_ref[start // steps + r, :, there] = total[r * steps : (r + 1) * steps].astype(bf16)
            at += width
    copy = pltpu.make_async_copy(done_ref, out_ref.at[:, :, here_columns], sem)
    copy.start()
    copy.wait()


def finish(finals, widths, first, low, got, ups, table, held_out, steps, columns, per_block):
    total, rank = low.shape
    wide = sum(widths)
    operands = [a for addends in finals for a, _ in addends] + [low, got, *ups]
    in_specs = [pl.BlockSpec(memory_space=pltpu.SMEM)] * len(table)
    in_specs += [pl.BlockSpec(memory_space=pltpu.VMEM)] * len(operands)
    aliases = {}
    if held_out is not None:
        aliases = {len(table) + len(operands): 0}
        operands.append(held_out)
        in_specs.append(pl.BlockSpec(memory_space=pl.ANY))
    return pl.pallas_call(
        functools.partial(
            finish_kernel,
            offsets=[[off for _, off in addends] for addends in finals],
            widths=widths,
            first=first,
            n_rep=len(ups),
            per_block=per_block,
            held=ups[0].shape[0],
        ),
        in_specs=in_specs,
        out_specs=pl.BlockSpec(memory_space=pl.ANY),
        out_shape=jax.ShapeDtypeStruct((total // steps, steps, columns), bf16),
        scratch_shapes=[
            pltpu.VMEM((total, wide), f32),
            pltpu.VMEM((total // steps, steps, wide), bf16),
            pltpu.SemaphoreType.DMA,
        ],
        input_output_aliases=aliases,
        compiler_params=pltpu.CompilerParams(vmem_limit_bytes=12 << 20),
        cost_estimate=hint,
        name="finish",
    )(*map(in_hbm, table), *operands)


def halving_order(n):
    if n == 1:
        return [0]
    rest = halving_order(n // 2)
    return [2 * u + 1 for u in rest] + [2 * u for u in rest]


def after(x, *others):
    return lax.optimization_barrier((x, *others))[0]


def on_device(
    queries,
    cached_key_store,
    cached_value_store,
    decode_step_keys,
    decode_step_values,
    request_cache_length,
    output_projection_weight,
    adapter_down_weight,
    adapter_up_weight,
    adapter_store_slot,
    adapter_ranks,
    request_block_adapter,
):
    n_tp, n_rep = lax.axis_size("tp"), lax.axis_size("rep")
    me = lax.axis_index("tp")[None].astype(jnp.int32)
    my_rep = lax.axis_index("rep")[None].astype(jnp.int32)
    reqs, steps, width = queries.shape
    blocks = request_block_adapter.shape[0]
    columns = width // n_tp
    per_block = reqs * n_tp * steps // blocks
    table = (my_rep, request_block_adapter, adapter_store_slot, adapter_ranks)

    arrays = (
        queries,
        cached_key_store,
        cached_value_store,
        decode_step_keys,
        decode_step_values,
        request_cache_length,
    )
    order = halving_order(n_tp)
    eighth = columns // 8
    widths = [4 * eighth, 3 * eighth, 1 * eighth] if eighth % lanes == 0 else [columns // 2] * 2
    parts = len(widths)
    starts = [sum(widths[:q]) for q in range(parts)]
    owners = n_tp // 2
    top_bit = n_rep // 2

    def relay(x, across, go):
        held = {0: after(x, go), top_bit: after(across, go)}
        bit = top_bit // 2
        while bit >= 1:
            for p in list(held):
                held[p ^ bit] = swap(held[p], "rep", bit)
            bit //= 2
        return [held[p] for p in range(n_rep)]

    down_across = swap(adapter_down_weight, "rep", top_bit)
    far, near = range(1, n_tp), range(1)
    own = dict(zip(far, attend(*arrays, me, far, n_tp)))
    pieces = {p: swap(own[p], "tp", p) for p in reversed(far)}
    own.update(zip(near, attend(*arrays, me, near, n_tp, [own[n_tp - 1]])))
    pieces[0] = own[0]
    weight = load(output_projection_weight, me, order[:owners], widths[0], columns, [own[0]])

    send, x = project([pieces[p] for p in range(n_tp)], weight, me)
    downs = relay(adapter_down_weight, down_across, send)
    up_across = swap(after(adapter_up_weight, send), "rep", top_bit)
    *sends, keep, low = project_rest(
        x, output_projection_weight, downs, me, table, order, widths, columns, per_block
    )
    gots = [swap(send, "tp", 1) for send in (send, *sends)]
    finals, last = [], [keep]
    for q in range(parts):
        addends = [(keep, owners * starts[q]), (gots[q], 0)]
        wide = owners * widths[q]
        bit = 2
        while bit < n_tp:
            wide //= 2
            out = combine(addends, wide, low if q == 1 else None, last)
            if q == 1:
                low = out[1]
            got = swap(out[0], "tp", bit)
            if bit == 2:
                last = [out[0]]
            addends = [(a, off + wide) for a, off in addends] + [(got, 0)]
            bit *= 2
        finals.append(addends)
        if q == 0:
            ups = relay(adapter_up_weight, up_across, last[0])
        if q == 1:
            low_parts = (low, got)

    result = None
    for group in (slice(0, parts - 1), slice(parts - 1, parts)):
        result = finish(
            finals[group],
            widths[group],
            starts[group.start],
            *low_parts,
            ups,
            table,
            result,
            steps,
            columns,
            per_block,
        )
    return result


def solution(mesh):
    placed = (
        P(("parts", "rep", "tp"), None, None),
        P(("parts", "rep", "tp"), None, None, None),
        P(("parts", "rep", "tp"), None, None, None),
        P(("parts", "rep", "tp"), None, None, None),
        P(("parts", "rep", "tp"), None, None, None),
        P(("parts", "rep", "tp")),
        P("tp", None),
        P("rep", "tp", None),
        P("rep", None, "tp"),
        P(),
        P(),
        P("rep"),
    )
    return jax.shard_map(
        on_device,
        mesh=mesh,
        in_specs=placed,
        out_specs=P(("parts", "rep"), None, "tp"),
        check_vma=False,
    )
```

profile of v0, /device:TPU:0, one launch (start us, length us, event | category | flops | bytes accessed | tf_op | source)
XLA Modules:
  0.0 72.9 jit_solution(15793154417082443212)
XLA Ops:
  0.0 2.9 %collective-permute-start.4 = (bf16[2,1024,128]{2,1,0:T(8,128)(2,1)}, bf16[2,1024,128]{2,1,0:T(8,128)(2,1)S(1)}, u32[]{:S(2)}, u32[]{:S(2)}) collective-permute-start(bf16[2,1024,128]{2,1,0:T(8,128)(2,1)} %refs_6_), channel_id=1, source_target_pairs={{0,8},{4,12},{8,0},{12,4},{1,9},{5,13},{9,1},{13,5},{2,10},{6,14},... | collective-permute-start | bytes 1572872 | tf_op jit(solution)/shard_map/ppermute | solution.py:20
  2.9 4.0 %attention.2 = (bf16[64,1024]{1,0:T(8,128)(2,1)S(1)}, bf16[64,1024]{1,0:T(8,128)(2,1)S(1)}, bf16[64,1024]{1,0:T(8,128)(2,1)S(1)}) custom-call(s32[1]{0:T(128)} %bitcast.1.me_ref, s32[16]{0:T(128)} %len_ref.3, bf16[16,4,4096]{2,1,0:T(4,128)(2,1)} %q_ref.3, bf16[16,4,4,128]{3,2,1,0:T(4,128)(2,1)} %dk_ref.3, bf16[16,4,4,128]{3,2,1,0:T(4,128)(2,1)} %dv_ref.3, ...), custom_call_target="tpu_custom_call" | custom-call | flops 1 | bytes 1 | tf_op jit(solution)/shard_map/attention/pallas_call | solution.py:122
  6.9 1.6 %collective-permute-start = (bf16[64,1024]{1,0:T(8,128)(2,1)S(1)}, bf16[64,1024]{1,0:T(8,128)(2,1)S(1)}, u32[]{:S(2)}, u32[]{:S(2)}) collective-permute-start(bf16[64,1024]{1,0:T(8,128)(2,1)S(1)} %get-tuple-element.22), channel_id=1, source_target_pairs={{0,1},{1,0},{2,3},{3,2},{4,5},{5,4},{6,7},{7,6},{8,9},{9,8},{10,11... | collective-permute-start | bytes 393224 | tf_op jit(solution)/shard_map/ppermute | solution.py:20
  8.6 2.6 %collective-permute-start.1 = (bf16[64,1024]{1,0:T(8,128)(2,1)S(1)}, bf16[64,1024]{1,0:T(8,128)(2,1)S(1)}, u32[]{:S(2)}, u32[]{:S(2)}) collective-permute-start(bf16[64,1024]{1,0:T(8,128)(2,1)S(1)} %get-tuple-element.23), channel_id=1, source_target_pairs={{0,2},{1,3},{2,0},{3,1},{4,6},{5,7},{6,4},{7,5},{8,10},{9,11},{10,... | collective-permute-start | bytes 393224 | tf_op jit(solution)/shard_map/ppermute | solution.py:20
  11.4 2.9 %attention.3.refs_0_ = bf16[64,1024]{1,0:T(8,128)(2,1)S(1)} custom-call(s32[1]{0:T(128)} %bitcast.1.me_ref, s32[16]{0:T(128)} %len_ref.3, bf16[16,4,4096]{2,1,0:T(4,128)(2,1)} %q_ref.3, bf16[16,4,4,128]{3,2,1,0:T(4,128)(2,1)} %dk_ref.3, bf16[16,4,4,128]{3,2,1,0:T(4,128)(2,1)} %dv_ref.3, bf16[16,4,128,128]{3,2,1,0:T(8,128)(2,1)} %refs_0_.3, ...), custom_call_target="tpu_custom_call" | custom-call | flops 1 | bytes 1 | tf_op jit(solution)/shard_map/attention/pallas_call | solution.py:122
  14.3 1.6 %load.1.refs_4_ = bf16[1024,1024]{1,0:T(8,128)(2,1)S(1)} custom-call(s32[1]{0:T(128)} %bitcast.1.me_ref, bf16[1024,4096]{1,0:T(8,128)(2,1)} %refs_5_.3, bf16[64,1024]{1,0:T(8,128)(2,1)S(1)} %attention.3.refs_0_), custom_call_target="tpu_custom_call" | custom-call | flops 1 | bytes 1 | tf_op jit(solution)/shard_map/load/pallas_call | solution.py:165
  15.9 5.3 %collective-permute-done.1.refs_2_ = bf16[64,1024]{1,0:T(8,128)(2,1)S(1)} collective-permute-done((bf16[64,1024]{1,0:T(8,128)(2,1)S(1)}, bf16[64,1024]{1,0:T(8,128)(2,1)S(1)}, u32[]{:S(2)}, u32[]{:S(2)}) %collective-permute-start.1) | collective-permute-done | bytes 131104 | tf_op jit(solution)/shard_map/ppermute | solution.py:20
  21.2 1.5 %projection.1 = (bf16[256,1024]{1,0:T(8,128)(2,1)}, bf16[256,1024]{1,0:T(8,128)(2,1)S(1)}) custom-call(s32[1]{0:T(128)} %bitcast.1.me_ref, bf16[64,1024]{1,0:T(8,128)(2,1)S(1)} %attention.3.refs_0_, bf16[64,1024]{1,0:T(8,128)(2,1)S(1)} %collective-permute-done.refs_1_, bf16[64,1024]{1,0:T(8,128)(2,1)S(1)} %collective-permute-done.1.refs_2_, ...), custom_call_target="tpu_custom_call" | custom-call | flops 1 | bytes 1 | tf_op jit(solution)/shard_map/projection/pallas_call | solution.py:195
  23.3 2.0 %collective-permute-start.7 = (bf16[256,1024]{1,0:T(8,128)(2,1)}, bf16[256,1024]{1,0:T(8,128)(2,1)S(1)}, u32[]{:S(2)}, u32[]{:S(2)}) collective-permute-start(bf16[256,1024]{1,0:T(8,128)(2,1)} %get-tuple-element.25), channel_id=1, source_target_pairs={{0,1},{1,0},{2,3},{3,2},{4,5},{5,4},{6,7},{7,6},{8,9},{9,8},{10,11... | collective-permute-start | bytes 1572872 | tf_op jit(solution)/shard_map/ppermute | solution.py:20
  25.2 0.5 collective-permute-start.12
  25.8 5.7 %projection_rest.1 = (bf16[256,896]{1,0:T(8,128)(2,1)S(1)}, bf16[256,256]{1,0:T(8,128)(2,1)S(1)}, bf16[256,2048]{1,0:T(8,128)(2,1)S(1)}, f32[256,128]{1,0:T(8,128)S(1)}) custom-call(s32[1]{0:T(128)} %bitcast.1.me_ref, s32[1]{0:T(128)} %bitcast.refs_0_, s32[4]{0:T(128)} %refs_1_.9, s32[8]{0:T(128)} %refs_2_.7, s32[8]{0:T(128)} %refs_3_.7, ...), custom_call_target="tpu_custom_call" | custom-call | flops 1 | bytes 1 | tf_op jit(solution)/shard_map/projection_rest/pallas_call | solution.py:254
  31.5 1.8 %collective-permute-start.8 = (bf16[256,896]{1,0:T(8,128)(2,1)S(1)}, bf16[256,896]{1,0:T(8,128)(2,1)S(1)}, u32[]{:S(2)}, u32[]{:S(2)}) collective-permute-start(bf16[256,896]{1,0:T(8,128)(2,1)S(1)} %get-tuple-element.30), channel_id=1, source_target_pairs={{0,1},{1,0},{2,3},{3,2},{4,5},{5,4},{6,7},{7,6},{8,9},{9,8},{10,11... | collective-permute-start | bytes 1376264 | tf_op jit(solution)/shard_map/ppermute | solution.py:20
  33.3 5.0 %collective-permute-done.7.refs_2_.refs_5_ = bf16[256,1024]{1,0:T(8,128)(2,1)S(1)} collective-permute-done((bf16[256,1024]{1,0:T(8,128)(2,1)}, bf16[256,1024]{1,0:T(8,128)(2,1)S(1)}, u32[]{:S(2)}, u32[]{:S(2)}) %collective-permute-start.7) | collective-permute-done | bytes 524320 | tf_op jit(solution)/shard_map/ppermute | solution.py:20
  38.3 0.6 collective-permute-done.12.refs_14_.refs_11_
  38.9 0.5 collective-permute-start.13
  39.4 2.5 %collective-permute-start.14 = (bf16[256,512]{1,0:T(8,128)(2,1)S(1)}, bf16[256,512]{1,0:T(8,128)(2,1)S(1)}, u32[]{:S(2)}, u32[]{:S(2)}) collective-permute-start(bf16[256,512]{1,0:T(8,128)(2,1)S(1)} %combine.3.refs_0_), channel_id=1, source_target_pairs={{0,2},{1,3},{2,0},{3,1},{4,6},{5,7},{6,4},{7,5},{8,10},{9,11},{10,... | collective-permute-start | bytes 786440 | tf_op jit(solution)/shard_map/ppermute | solution.py:20
  41.9 11.1 %collective-permute-done.8.refs_2_.refs_8_ = bf16[256,896]{1,0:T(8,128)(2,1)S(1)} collective-permute-done((bf16[256,896]{1,0:T(8,128)(2,1)S(1)}, bf16[256,896]{1,0:T(8,128)(2,1)S(1)}, u32[]{:S(2)}, u32[]{:S(2)}) %collective-permute-start.8) | collective-permute-done | bytes 458784 | tf_op jit(solution)/shard_map/ppermute | solution.py:20
  53.1 0.6 collective-permute-start.10
  53.8 2.5 %collective-permute-start.6 = (bf16[256,256]{1,0:T(8,128)(2,1)S(1)}, bf16[256,256]{1,0:T(8,128)(2,1)S(1)}, u32[]{:S(2)}, u32[]{:S(2)}) collective-permute-start(bf16[256,256]{1,0:T(8,128)(2,1)S(1)} %get-tuple-element.29), channel_id=1, source_target_pairs={{0,1},{1,0},{2,3},{3,2},{4,5},{5,4},{6,7},{7,6},{8,9},{9,8},{10,11... | collective-permute-start | bytes 393224 | tf_op jit(solution)/shard_map/ppermute | solution.py:20
  56.2 5.6 %collective-permute-done.6.refs_2_.refs_5_ = bf16[256,256]{1,0:T(8,128)(2,1)S(1)} collective-permute-done((bf16[256,256]{1,0:T(8,128)(2,1)S(1)}, bf16[256,256]{1,0:T(8,128)(2,1)S(1)}, u32[]{:S(2)}, u32[]{:S(2)}) %collective-permute-start.6) | collective-permute-done | bytes 131104 | tf_op jit(solution)/shard_map/ppermute | solution.py:20
  61.9 3.3 %collective-permute-start.9 = (bf16[256,128]{1,0:T(8,128)(2,1)S(1)}, bf16[256,128]{1,0:T(8,128)(2,1)S(1)}, u32[]{:S(2)}, u32[]{:S(2)}) collective-permute-start(bf16[256,128]{1,0:T(8,128)(2,1)S(1)} %combine.5), channel_id=1, source_target_pairs={{0,2},{1,3},{2,0},{3,1},{4,6},{5,7},{6,4},{7,5},{8,10},{9,11},{10,... | collective-permute-start | bytes 196616 | tf_op jit(solution)/shard_map/ppermute | solution.py:20
  65.2 2.9 %collective-permute-done.10.refs_9_.refs_11_.refs_8_ = bf16[256,512]{1,0:T(8,128)(2,1)S(1)} collective-permute-done((bf16[256,512]{1,0:T(8,128)(2,1)S(1)}, bf16[256,512]{1,0:T(8,128)(2,1)S(1)}, u32[]{:S(2)}, u32[]{:S(2)}) %collective-permute-start.10) | collective-permute-done | bytes 262176 | tf_op jit(solution)/shard_map/ppermute | solution.py:20
  68.1 2.7 %finish.2.refs_13_ = bf16[64,4,1024]{2,1,0:T(4,128)(2,1)} custom-call(s32[1]{0:T(128)} %bitcast.refs_0_, s32[4]{0:T(128)} %refs_1_.9, s32[8]{0:T(128)} %refs_2_.7, s32[8]{0:T(128)} %refs_3_.7, bf16[256,2048]{1,0:T(8,128)(2,1)S(1)} %get-tuple-element.28.refs_0_.refs_1_.refs_4_.refs_7_, bf16[256,1024]{1,0:T(8,128)(2,1)S(1)} %collective-permute-done.7.refs_2_.refs_5_, ...), custom_call_target="tpu_custom_call" | custom-call | flops 1 | bytes 1 | tf_op jit(solution)/shard_map/finish/pallas_call | solution.py:372
  70.8 2.1 %finish.3 = bf16[64,4,1024]{2,1,0:T(4,128)(2,1)} custom-call(s32[1]{0:T(128)} %bitcast.refs_0_, s32[4]{0:T(128)} %refs_1_.9, s32[8]{0:T(128)} %refs_2_.7, s32[8]{0:T(128)} %refs_3_.7, bf16[256,2048]{1,0:T(8,128)(2,1)S(1)} %get-tuple-element.28.refs_0_.refs_1_.refs_4_.refs_7_, ...), custom_call_target="tpu_custom_call", output_to_operand_aliasing={{}: (13, {})} | custom-call | flops 1 | bytes 1 | tf_op jit(solution)/shard_map/finish/pallas_call | solution.py:372
  (20 shorter events, 0.9 us)
Async XLA Ops:
  0.0 22.8 %collective-permute-start.4 = (bf16[2,1024,128]{2,1,0:T(8,128)(2,1)}, bf16[2,1024,128]{2,1,0:T(8,128)(2,1)S(1)}, u32[]{:S(2)}, u32[]{:S(2)}) collective-permute-start(bf16[2,1024,128]{2,1,0:T(8,128)(2,1)} %refs_6_), channel_id=1, source_target_pairs={{0,8},{4,12},{8,0},{12,4},{1,9},{5,13},{9,1},{13,5},{2,10},{6,14},... | collective-permute-start | bytes 1572872 | tf_op jit(solution)/shard_map/ppermute | solution.py:20
  6.9 8.9 %collective-permute-start = (bf16[64,1024]{1,0:T(8,128)(2,1)S(1)}, bf16[64,1024]{1,0:T(8,128)(2,1)S(1)}, u32[]{:S(2)}, u32[]{:S(2)}) collective-permute-start(bf16[64,1024]{1,0:T(8,128)(2,1)S(1)} %get-tuple-element.22), channel_id=1, source_target_pairs={{0,1},{1,0},{2,3},{3,2},{4,5},{5,4},{6,7},{7,6},{8,9},{9,8},{10,11... | collective-permute-start | bytes 393224 | tf_op jit(solution)/shard_map/ppermute | solution.py:20
  8.6 12.6 %collective-permute-start.1 = (bf16[64,1024]{1,0:T(8,128)(2,1)S(1)}, bf16[64,1024]{1,0:T(8,128)(2,1)S(1)}, u32[]{:S(2)}, u32[]{:S(2)}) collective-permute-start(bf16[64,1024]{1,0:T(8,128)(2,1)S(1)} %get-tuple-element.23), channel_id=1, source_target_pairs={{0,2},{1,3},{2,0},{3,1},{4,6},{5,7},{6,4},{7,5},{8,10},{9,11},{10,... | collective-permute-start | bytes 393224 | tf_op jit(solution)/shard_map/ppermute | solution.py:20
  11.2 10.1 %collective-permute-start.2 = (bf16[64,1024]{1,0:T(8,128)(2,1)S(1)}, bf16[64,1024]{1,0:T(8,128)(2,1)S(1)}, u32[]{:S(2)}, u32[]{:S(2)}) collective-permute-start(bf16[64,1024]{1,0:T(8,128)(2,1)S(1)} %get-tuple-element.21.refs_2_), channel_id=1, source_target_pairs={{0,3},{1,2},{2,1},{3,0},{4,7},{5,6},{6,5},{7,4},{8,11},{9,10},{10,... | collective-permute-start | bytes 393224 | tf_op jit(solution)/shard_map/ppermute | solution.py:20
  15.9 6.9 %copy-start.1 = (bf16[2,1024,128]{2,1,0:T(8,128)(2,1)S(1)}, bf16[2,1024,128]{2,1,0:T(8,128)(2,1)}, u32[]{:S(2)}) copy-start(bf16[2,1024,128]{2,1,0:T(8,128)(2,1)} %refs_6_) | copy-start | bytes 1572868
  15.9 9.4 %copy-start = (bf16[2,128,1024]{2,1,0:T(8,128)(2,1)S(1)}, bf16[2,128,1024]{2,1,0:T(8,128)(2,1)}, u32[]{:S(2)}) copy-start(bf16[2,128,1024]{2,1,0:T(8,128)(2,1)} %refs_9_) | copy-start | bytes 1572868
  22.8 3.0 %collective-permute-start.3 = (bf16[2,1024,128]{2,1,0:T(8,128)(2,1)S(1)}, bf16[2,1024,128]{2,1,0:T(8,128)(2,1)}, u32[]{:S(2)}, u32[]{:S(2)}) collective-permute-start(bf16[2,1024,128]{2,1,0:T(8,128)(2,1)S(1)} %copy-done.1), channel_id=1, source_target_pairs={{0,4},{4,0},{8,12},{12,8},{1,5},{5,1},{9,13},{13,9},{2,6},{6,2},{1... | collective-permute-start | bytes 1572872 | tf_op jit(solution)/shard_map/ppermute | solution.py:20
  22.8 3.0 %collective-permute-start.5 = (bf16[2,1024,128]{2,1,0:T(8,128)(2,1)S(1)}, bf16[2,1024,128]{2,1,0:T(8,128)(2,1)}, u32[]{:S(2)}, u32[]{:S(2)}) collective-permute-start(bf16[2,1024,128]{2,1,0:T(8,128)(2,1)S(1)} %collective-permute-done.4.refs_8_), channel_id=1, source_target_pairs={{0,4},{4,0},{8,12},{12,8},{1,5},{5,1},{9,13},{13,9},{2,6},{6,2},{1... | collective-permute-start | bytes 1572872 | tf_op jit(solution)/shard_map/ppermute | solution.py:20
  23.3 15.0 %collective-permute-start.7 = (bf16[256,1024]{1,0:T(8,128)(2,1)}, bf16[256,1024]{1,0:T(8,128)(2,1)S(1)}, u32[]{:S(2)}, u32[]{:S(2)}) collective-permute-start(bf16[256,1024]{1,0:T(8,128)(2,1)} %get-tuple-element.25), channel_id=1, source_target_pairs={{0,1},{1,0},{2,3},{3,2},{4,5},{5,4},{6,7},{7,6},{8,9},{9,8},{10,11... | collective-permute-start | bytes 1572872 | tf_op jit(solution)/shard_map/ppermute | solution.py:20
  25.2 13.6 %collective-permute-start.12 = (bf16[2,128,1024]{2,1,0:T(8,128)(2,1)S(1)}, bf16[2,128,1024]{2,1,0:T(8,128)(2,1)S(1)}, u32[]{:S(2)}, u32[]{:S(2)}) collective-permute-start(bf16[2,128,1024]{2,1,0:T(8,128)(2,1)S(1)} %copy-done), channel_id=1, source_target_pairs={{0,8},{4,12},{8,0},{12,4},{1,9},{5,13},{9,1},{13,5},{2,10},{6,14},... | collective-permute-start | bytes 1572872 | tf_op jit(solution)/shard_map/ppermute | solution.py:20
  31.5 21.6 %collective-permute-start.8 = (bf16[256,896]{1,0:T(8,128)(2,1)S(1)}, bf16[256,896]{1,0:T(8,128)(2,1)S(1)}, u32[]{:S(2)}, u32[]{:S(2)}) collective-permute-start(bf16[256,896]{1,0:T(8,128)(2,1)S(1)} %get-tuple-element.30), channel_id=1, source_target_pairs={{0,1},{1,0},{2,3},{3,2},{4,5},{5,4},{6,7},{7,6},{8,9},{9,8},{10,11... | collective-permute-start | bytes 1376264 | tf_op jit(solution)/shard_map/ppermute | solution.py:20
  38.9 26.3 %collective-permute-start.11 = (bf16[2,128,1024]{2,1,0:T(8,128)(2,1)S(1)}, bf16[2,128,1024]{2,1,0:T(8,128)(2,1)S(1)}, u32[]{:S(2)}, u32[]{:S(2)}) collective-permute-start(bf16[2,128,1024]{2,1,0:T(8,128)(2,1)S(1)} %copy-done), channel_id=1, source_target_pairs={{0,4},{4,0},{8,12},{12,8},{1,5},{5,1},{9,13},{13,9},{2,6},{6,2},{1... | collective-permute-start | bytes 1572872 | tf_op jit(solution)/shard_map/ppermute | solution.py:20
  38.9 26.3 %collective-permute-start.13 = (bf16[2,128,1024]{2,1,0:T(8,128)(2,1)S(1)}, bf16[2,128,1024]{2,1,0:T(8,128)(2,1)S(1)}, u32[]{:S(2)}, u32[]{:S(2)}) collective-permute-start(bf16[2,128,1024]{2,1,0:T(8,128)(2,1)S(1)} %collective-permute-done.12.refs_14_.refs_11_), channel_id=1, source_target_pairs={{0,4},{4,0},{8,12},{12,8},{1,5},{5,1},{9,13},{13,9},{2,6},{6,2},{1... | collective-permute-start | bytes 1572872 | tf_op jit(solution)/shard_map/ppermute | solution.py:20
  39.4 25.8 %collective-permute-start.14 = (bf16[256,512]{1,0:T(8,128)(2,1)S(1)}, bf16[256,512]{1,0:T(8,128)(2,1)S(1)}, u32[]{:S(2)}, u32[]{:S(2)}) collective-permute-start(bf16[256,512]{1,0:T(8,128)(2,1)S(1)} %combine.3.refs_0_), channel_id=1, source_target_pairs={{0,2},{1,3},{2,0},{3,1},{4,6},{5,7},{6,4},{7,5},{8,10},{9,11},{10,... | collective-permute-start | bytes 786440 | tf_op jit(solution)/shard_map/ppermute | solution.py:20
  53.1 15.0 %collective-permute-start.10 = (bf16[256,512]{1,0:T(8,128)(2,1)S(1)}, bf16[256,512]{1,0:T(8,128)(2,1)S(1)}, u32[]{:S(2)}, u32[]{:S(2)}) collective-permute-start(bf16[256,512]{1,0:T(8,128)(2,1)S(1)} %get-tuple-element.32.refs_0_), channel_id=1, source_target_pairs={{0,2},{1,3},{2,0},{3,1},{4,6},{5,7},{6,4},{7,5},{8,10},{9,11},{10,... | collective-permute-start | bytes 786440 | tf_op jit(solution)/shard_map/ppermute | solution.py:20
  53.8 8.1 %collective-permute-start.6 = (bf16[256,256]{1,0:T(8,128)(2,1)S(1)}, bf16[256,256]{1,0:T(8,128)(2,1)S(1)}, u32[]{:S(2)}, u32[]{:S(2)}) collective-permute-start(bf16[256,256]{1,0:T(8,128)(2,1)S(1)} %get-tuple-element.29), channel_id=1, source_target_pairs={{0,1},{1,0},{2,3},{3,2},{4,5},{5,4},{6,7},{7,6},{8,9},{9,8},{10,11... | collective-permute-start | bytes 393224 | tf_op jit(solution)/shard_map/ppermute | solution.py:20
  61.9 8.9 %collective-permute-start.9 = (bf16[256,128]{1,0:T(8,128)(2,1)S(1)}, bf16[256,128]{1,0:T(8,128)(2,1)S(1)}, u32[]{:S(2)}, u32[]{:S(2)}) collective-permute-start(bf16[256,128]{1,0:T(8,128)(2,1)S(1)} %combine.5), channel_id=1, source_target_pairs={{0,2},{1,3},{2,0},{3,1},{4,6},{5,7},{6,4},{7,5},{8,10},{9,11},{10,... | collective-permute-start | bytes 196616 | tf_op jit(solution)/shard_map/ppermute | solution.py:20
where the time goes:
time: 73.1 us; the launch traced here: 72.9 us
  waiting for transfers between devices  30.6 us (42%)
  starting transfers between devices  21.6 us (30%)
  Pallas kernels  20.6 us (28%)
    ppermute x15, waiting for transfers between devices, swap(): return lax.ppermute(x, axis, [(i, i ^ bit) for i in range(n)])  30.6 us
    ppermute x15, starting transfers between devices, swap(): return lax.ppermute(x, axis, [(i, i ^ bit) for i in range(n)])  21.6 us
    pallas_call x2, Pallas kernels, attend(): pl.pallas_call(functools.partial(attend_kernel, pieces=pieces, n_tp=n_tp,...  6.87 us
    pallas_call x1, Pallas kernels, project_rest(): pl.pallas_call(functools.partial(project_rest_kernel, order=order, widths...  5.65 us
    pallas_call x2, Pallas kernels, finish(): pl.pallas_call(functools.partial(finish_kernel, offsets=[[off for _, off...  4.78 us
    pallas_call x1, Pallas kernels, load(): pl.pallas_call(functools.partial(load_kernel, owners=owners, part=part, c...  1.57 us
    pallas_call x1, Pallas kernels, project(): pl.pallas_call(project_kernel, in_specs=[pl.BlockSpec(memory_space=pltpu....  1.54 us
  transfers between devices with their start and end apart: 15, of which 6 were waited for; matrix products, arithmetic and copies ran while one was open for 0% of the time, Pallas kernels for 25%

commit v1 on v0

--- a/solution.py
+++ b/solution.py
@@ -13,6 +13,7 @@
 f32 = jnp.float32
 bf16 = jnp.bfloat16
 hint = pl.CostEstimate(flops=1, bytes_accessed=1, transcendentals=0)
+long = pl.CostEstimate(flops=10**11, bytes_accessed=10**9, transcendentals=0)
 
 
 def swap(x, axis, bit):
@@ -202,19 +203,17 @@
             jax.ShapeDtypeStruct((total, pieces[0].shape[1]), bf16),
         ],
         compiler_params=pltpu.CompilerParams(vmem_limit_bytes=8 << 20),
-        cost_estimate=hint,
+        cost_estimate=long,
         name="projection",
     )(me, *pieces, in_vmem(weight))
 
 
-def project_rest_kernel(me_ref, *refs, order, widths, columns, adapters, per_block, held):
-    table, refs = (*refs[:4], held), refs[4:]
-    x_ref, w_ref, downs, refs = refs[0], refs[1], refs[2 : 2 + adapters], refs[2 + adapters :]
+def project_rest_kernel(me_ref, x_ref, w_ref, *refs, order, widths, columns):
     parts, owners = len(widths), len(order) // 2
-    outs, keep_ref, low_ref = refs[: parts - 1], refs[parts - 1], refs[parts]
-    nears, sems = refs[parts + 1 : -1], refs[-1]
+    outs, keep_ref = refs[: parts - 2], refs[parts - 2]
+    nears, sems = refs[parts - 1 : -1], refs[-1]
     starts = [sum(widths[:q]) for q in range(parts)]
-    jobs = [(order[:owners], q) for q in range(1, parts)] + [(order[owners:], q) for q in range(parts)]
+    jobs = [(order[:owners], q) for q in range(1, parts - 1)] + [(order[owners:], q) for q in range(parts)]
     copies = [
         weight_copies(me_ref[0], w_ref, near, sems.at[h], relative, columns, starts[q], widths[q])
         for h, (near, (relative, q)) in enumerate(zip(nears, jobs))
@@ -222,6 +221,41 @@
     for group in copies:
         for copy in group:
             copy.start()
+    for h, (near, (_, q)) in enumerate(zip(nears, jobs)):
+        for copy in copies[h]:
+            copy.wait()
+        got = jnp.dot(x_ref[...], near[...], preferred_element_type=f32).astype(bf16)
+        if h < parts - 2:
+            outs[h][...] = got
+        else:
+            keep_ref[:, owners * starts[q] : owners * (starts[q] + widths[q])] = got
+
+
+def project_rest(x, weight, me, order, widths, columns):
+    rows, feats = x.shape
+    parts, owners = len(widths), len(order) // 2
+    vmem = pl.BlockSpec(memory_space=pltpu.VMEM)
+    return pl.pallas_call(
+        functools.partial(project_rest_kernel, order=order, widths=widths, columns=columns),
+        in_specs=[pl.BlockSpec(memory_space=pltpu.SMEM), vmem, pl.BlockSpec(memory_space=pl.ANY)],
+        out_specs=[vmem] * (parts - 1),
+        out_shape=[jax.ShapeDtypeStruct((rows, owners * w), bf16) for w in (*widths[1:-1], columns)],
+        scratch_shapes=[pltpu.VMEM((feats, owners * w), weight.dtype) for w in (*widths[1:-1], *widths)]
+        + [pltpu.SemaphoreType.DMA((2 * parts - 2, owners))],
+        compiler_params=pltpu.CompilerParams(vmem_limit_bytes=20 << 20),
+        cost_estimate=hint,
+        name="projection_rest",
+    )(me, x, in_hbm(weight))
+
+
+def project_last_kernel(me_ref, *refs, owners, width, columns, adapters, per_block, held, waits):
+    table, refs = (*refs[:4], held), refs[4:]
+    x_ref, w_ref, downs = refs[0], refs[1], refs[2 : 2 + adapters]
+    out_ref, low_ref, near, sems = refs[2 + adapters + waits :]
+    copies = weight_copies(me_ref[0], w_ref, near, sems, owners, columns, columns - width, width)
+    for copy in copies:
+        copy.start()
+    wide = len(owners) * width
     for start in range(0, x_ref.shape[0], per_block):
         home, place, _ = block_place(table, start // per_block)
         here = slice(start, start + per_block)
@@ -231,48 +265,46 @@
             def _():
                 got = jnp.dot(x_ref[here, :], downs[i][place], preferred_element_type=f32)
                 low_ref[here, :] = got
-                outs[0][here, owners * widths[1] :] = got.astype(bf16)
-
-    for h, (near, (_, q)) in enumerate(zip(nears, jobs)):
-        for copy in copies[h]:
-            copy.wait()
-        got = jnp.dot(x_ref[...], near[...], preferred_element_type=f32).astype(bf16)
-        wide = owners * widths[q]
-        if h < parts - 1:
-            outs[h][:, :wide] = got
-        else:
-            keep_ref[:, owners * starts[q] : owners * starts[q] + wide] = got
-
-
-def project_rest(x, weight, downs, me, table, order, widths, columns, per_block):
+                out_ref[here, wide:] = got.astype(bf16)
+
+    for copy in copies:
+        copy.wait()
+    out_ref[:, :wide] = jnp.dot(x_ref[...], near[...], preferred_element_type=f32).astype(bf16)
+
+
+def project_last(x, weight, downs, me, table, owners, width, columns, per_block, waits):
     rows, feats = x.shape
-    parts, owners = len(widths), len(order) // 2
     held, _, rank = downs[0].shape
-    shapes = [(rows, owners * w) for w in (*widths[1:], columns)]
-    shapes[0] = (rows, owners * widths[1] + rank)
+    wide = len(owners) * width
     vmem = pl.BlockSpec(memory_space=pltpu.VMEM)
     return pl.pallas_call(
         functools.partial(
-            project_rest_kernel,
-            order=order,
-            widths=widths,
+            project_last_kernel,
+            owners=owners,
+            width=width,
             columns=columns,
             adapters=len(downs),
             per_block=per_block,
             held=held,
+            waits=len(waits),
         ),
         in_specs=[pl.BlockSpec(memory_space=pltpu.SMEM)] * (1 + len(table))
         + [vmem, pl.BlockSpec(memory_space=pl.ANY)]
-        + [vmem] * len(downs),
-        out_specs=[vmem] * (parts + 1),
-        out_shape=[jax.ShapeDtypeStruct(shape, bf16) for shape in shapes]
-        + [jax.ShapeDtypeStruct((rows, rank), f32)],
-        scratch_shapes=[pltpu.VMEM((feats, owners * w), weight.dtype) for w in (*widths[1:], *widths)]
-        + [pltpu.SemaphoreType.DMA((2 * parts - 1, owners))],
-        compiler_params=pltpu.CompilerParams(vmem_limit_bytes=20 << 20),
+        + [vmem] * len(downs)
+        + [pl.BlockSpec(memory_space=pl.ANY)] * len(waits),
+        out_specs=[vmem] * 2,
+        out_shape=[
+            jax.ShapeDtypeStruct((rows, wide + rank), bf16),
+            jax.ShapeDtypeStruct((rows, rank), f32),
+        ],
+        scratch_shapes=[
+            pltpu.VMEM((feats, wide), weight.dtype),
+            pltpu.SemaphoreType.DMA((len(owners),)),
+        ],
+        compiler_params=pltpu.CompilerParams(vmem_limit_bytes=16 << 20),
         cost_estimate=hint,
-        name="projection_rest",
-    )(me, *map(in_hbm, table), x, in_hbm(weight), *downs)
+        name="projection_last",
+    )(me, *map(in_hbm, table), x, in_hbm(weight), *downs, *waits)
 
 
 def combine_kernel(*refs, offsets, wide, with_low, waits):
@@ -311,7 +343,7 @@
         out_specs=[pl.BlockSpec(memory_space=pltpu.VMEM)] * len(out_shape),
         out_shape=out_shape,
         compiler_params=pltpu.CompilerParams(vmem_limit_bytes=8 << 20),
-        cost_estimate=hint,
+        cost_estimate=long,
         name="combine",
     )(*waits, *arrays)
 
@@ -453,57 +485,56 @@
             bit //= 2
         return [held[p] for p in range(n_rep)]
 
-    down_across = swap(adapter_down_weight, "rep", top_bit)
     far, near = range(1, n_tp), range(1)
     own = dict(zip(far, attend(*arrays, me, far, n_tp)))
     pieces = {p: swap(own[p], "tp", p) for p in reversed(far)}
     own.update(zip(near, attend(*arrays, me, near, n_tp, [own[n_tp - 1]])))
     pieces[0] = own[0]
+    down_across = swap(after(adapter_down_weight, own[0]), "rep", top_bit)
     weight = load(output_projection_weight, me, order[:owners], widths[0], columns, [own[0]])
 
     send, x = project([pieces[p] for p in range(n_tp)], weight, me)
-    downs = relay(adapter_down_weight, down_across, send)
-    up_across = swap(after(adapter_up_weight, send), "rep", top_bit)
-    *sends, keep, low = project_rest(
-        x, output_projection_weight, downs, me, table, order, widths, columns, per_block
-    )
+    *sends, keep = project_rest(x, output_projection_weight, me, order, widths, columns)
+    up_across = swap(after(adapter_up_weight, keep), "rep", top_bit)
     gots = [swap(send, "tp", 1) for send in (send, *sends)]
-    finals, last = [], [keep]
+    finals, last = [], []
+    low = None
     for q in range(parts):
+        if q == parts - 1:
+            send, low = project_last(
+                x,
+                output_projection_weight,
+                downs,
+                me,
+                table,
+                order[:owners],
+                widths[q],
+                columns,
+                per_block,
+                last,
+            )
+            gots.append(swap(send, "tp", 1))
         addends = [(keep, owners * starts[q]), (gots[q], 0)]
         wide = owners * widths[q]
         bit = 2
         while bit < n_tp:
             wide //= 2
-            out = combine(addends, wide, low if q == 1 else None, last)
-            if q == 1:
+            first = bit == 2
+            waits = last + ([up_across] if q == 1 else []) + ([finals[q - 2][-1][0]] if q >= 2 else [])
+            out = combine(addends, wide, low, waits if first else [])
+            if first:
+                last = [out[0]]
+            if low is not None:
                 low = out[1]
             got = swap(out[0], "tp", bit)
-            if bit == 2:
-                last = [out[0]]
             addends = [(a, off + wide) for a, off in addends] + [(got, 0)]
             bit *= 2
         finals.append(addends)
         if q == 0:
+            downs = relay(adapter_down_weight, down_across, last[0])
+        if q == 1:
             ups = relay(adapter_up_weight, up_across, last[0])
-        if q == 1:
-            low_parts = (low, got)
-
-    result = None
-    for group in (slice(0, parts - 1), slice(parts - 1, parts)):
-        result = finish(
-            finals[group],
-            widths[group],
-            starts[group.start],
-            *low_parts,
-            ups,
-            table,
-            result,
-            steps,
-            columns,
-            per_block,
-        )
-    return result
+    return finish(finals, widths, 0, low, got, ups, table, None, steps, columns, per_block)
 
 
 def solution(mesh):

time: 73.1 us -> 68.9 us (0.943)
  starting transfers between devices: 21.6 us -> 17 us
  waiting for transfers between devices: 30.6 us -> 33.2 us
  Pallas kernels: 20.6 us -> 18.3 us
    ppermute x15, starting transfers between devices: 21.6 us -> 17 us  [swap(): return lax.ppermute(x, axis, [(i, i ^ bit) for i in range(n)])]
    ppermute x15, waiting for transfers between devices: 30.6 us -> 33.2 us  [swap(): return lax.ppermute(x, axis, [(i, i ^ bit) for i in range(n)])]
    pallas_call x0 -> x1, Pallas kernels: none -> 2.18 us  [project_last(): pl.pallas_call(functools.partial(project_last_kernel, owners=owners, widt...]
    pallas_call x2 -> x1, Pallas kernels: 4.78 us -> 2.74 us  [finish(): pl.pallas_call(functools.partial(finish_kernel, offsets=[[off for _, off...]
    pallas_call x1, Pallas kernels: 5.65 us -> 4.02 us  [project_rest(): pl.pallas_call(functools.partial(project_rest_kernel, order=order, widths...]
    pallas_call x1, Pallas kernels: 1.54 us -> 0.74 us  [project(): pl.pallas_call(project_kernel, in_specs=[pl.BlockSpec(memory_space=pltpu....]
  transfers between devices with their start and end apart: 15 -> 15, of which waited for: 6 -> 7; matrix products, arithmetic and copies ran while one was open for 0% -> 0% of each run, Pallas kernels for 25% -> 16%
where the time goes in v1:
time: 68.9 us; the launch traced here: 68.7 us
  waiting for transfers between devices  33.2 us (48%)
  Pallas kernels  18.3 us (27%)
  starting transfers between devices  17 us (25%)
    ppermute x15, waiting for transfers between devices, swap(): return lax.ppermute(x, axis, [(i, i ^ bit) for i in range(n)])  33.2 us
    ppermute x15, starting transfers between devices, swap(): return lax.ppermute(x, axis, [(i, i ^ bit) for i in range(n)])  17 us
    pallas_call x2, Pallas kernels, attend(): pl.pallas_call(functools.partial(attend_kernel, pieces=pieces, n_tp=n_tp,...  6.87 us
    pallas_call x1, Pallas kernels, project_rest(): pl.pallas_call(functools.partial(project_rest_kernel, order=order, widths...  4.02 us
    pallas_call x1, Pallas kernels, finish(): pl.pallas_call(functools.partial(finish_kernel, offsets=[[off for _, off...  2.74 us
    pallas_call x1, Pallas kernels, project_last(): pl.pallas_call(functools.partial(project_last_kernel, owners=owners, widt...  2.18 us
    pallas_call x1, Pallas kernels, load(): pl.pallas_call(functools.partial(load_kernel, owners=owners, part=part, c...  1.57 us
  transfers between devices with their start and end apart: 15, of which 7 were waited for; matrix products, arithmetic and copies ran while one was open for 0% of the time, Pallas kernels for 16%

profile of v1, /device:TPU:0, one launch (start us, length us, event | category | flops | bytes accessed | tf_op | source)
XLA Modules:
  0.0 68.7 jit_solution(12575346699918857415)
XLA Ops:
  0.0 4.0 %attention.2 = (bf16[64,1024]{1,0:T(8,128)(2,1)S(1)}, bf16[64,1024]{1,0:T(8,128)(2,1)S(1)}, bf16[64,1024]{1,0:T(8,128)(2,1)S(1)}) custom-call(s32[1]{0:T(128)} %bitcast.1.me_ref, s32[16]{0:T(128)} %len_ref.3, bf16[16,4,4096]{2,1,0:T(4,128)(2,1)} %q_ref.3, bf16[16,4,4,128]{3,2,1,0:T(4,128)(2,1)} %dk_ref.3, bf16[16,4,4,128]{3,2,1,0:T(4,128)(2,1)} %dv_ref.3, ...), custom_call_target="tpu_custom_call" | custom-call | flops 1 | bytes 1 | tf_op jit(solution)/shard_map/attention/pallas_call | solution.py:123
  4.0 3.1 %collective-permute-start = (bf16[64,1024]{1,0:T(8,128)(2,1)S(1)}, bf16[64,1024]{1,0:T(8,128)(2,1)S(1)}, u32[]{:S(2)}, u32[]{:S(2)}) collective-permute-start(bf16[64,1024]{1,0:T(8,128)(2,1)S(1)} %get-tuple-element.23), channel_id=1, source_target_pairs={{0,1},{1,0},{2,3},{3,2},{4,5},{5,4},{6,7},{7,6},{8,9},{9,8},{10,11... | collective-permute-start | bytes 393224 | tf_op jit(solution)/shard_map/ppermute | solution.py:21
  7.1 2.6 %collective-permute-start.1 = (bf16[64,1024]{1,0:T(8,128)(2,1)S(1)}, bf16[64,1024]{1,0:T(8,128)(2,1)S(1)}, u32[]{:S(2)}, u32[]{:S(2)}) collective-permute-start(bf16[64,1024]{1,0:T(8,128)(2,1)S(1)} %get-tuple-element.24), channel_id=1, source_target_pairs={{0,2},{1,3},{2,0},{3,1},{4,6},{5,7},{6,4},{7,5},{8,10},{9,11},{10,... | collective-permute-start | bytes 393224 | tf_op jit(solution)/shard_map/ppermute | solution.py:21
  9.7 2.9 %attention.3.refs_0_ = bf16[64,1024]{1,0:T(8,128)(2,1)S(1)} custom-call(s32[1]{0:T(128)} %bitcast.1.me_ref, s32[16]{0:T(128)} %len_ref.3, bf16[16,4,4096]{2,1,0:T(4,128)(2,1)} %q_ref.3, bf16[16,4,4,128]{3,2,1,0:T(4,128)(2,1)} %dk_ref.3, bf16[16,4,4,128]{3,2,1,0:T(4,128)(2,1)} %dv_ref.3, bf16[16,4,128,128]{3,2,1,0:T(8,128)(2,1)} %refs_0_.3, ...), custom_call_target="tpu_custom_call" | custom-call | flops 1 | bytes 1 | tf_op jit(solution)/shard_map/attention/pallas_call | solution.py:123
  12.6 1.6 %load.1.refs_4_ = bf16[1024,1024]{1,0:T(8,128)(2,1)S(1)} custom-call(s32[1]{0:T(128)} %bitcast.1.me_ref, bf16[1024,4096]{1,0:T(8,128)(2,1)} %refs_5_.3, bf16[64,1024]{1,0:T(8,128)(2,1)S(1)} %attention.3.refs_0_), custom_call_target="tpu_custom_call" | custom-call | flops 1 | bytes 1 | tf_op jit(solution)/shard_map/load/pallas_call | solution.py:166
  14.2 5.8 %collective-permute-done.1.refs_2_ = bf16[64,1024]{1,0:T(8,128)(2,1)S(1)} collective-permute-done((bf16[64,1024]{1,0:T(8,128)(2,1)S(1)}, bf16[64,1024]{1,0:T(8,128)(2,1)S(1)}, u32[]{:S(2)}, u32[]{:S(2)}) %collective-permute-start.1) | collective-permute-done | bytes 131104 | tf_op jit(solution)/shard_map/ppermute | solution.py:21
  20.0 0.7 %projection.1 = (bf16[256,1024]{1,0:T(8,128)(2,1)S(1)}, bf16[256,1024]{1,0:T(8,128)(2,1)S(1)}) custom-call(s32[1]{0:T(128)} %bitcast.1.me_ref, bf16[64,1024]{1,0:T(8,128)(2,1)S(1)} %attention.3.refs_0_, bf16[64,1024]{1,0:T(8,128)(2,1)S(1)} %collective-permute-done.refs_1_, bf16[64,1024]{1,0:T(8,128)(2,1)S(1)} %collective-permute-done.1.refs_2_, ...), custom_call_target="tpu_custom_call" | custom-call | flops 99999997952 | bytes 1000000000 | tf_op jit(solution)/shard_map/projection/pallas_call | solution.py:196
  20.8 2.0 %collective-permute-start.3 = (bf16[256,1024]{1,0:T(8,128)(2,1)S(1)}, bf16[256,1024]{1,0:T(8,128)(2,1)S(1)}, u32[]{:S(2)}, u32[]{:S(2)}) collective-permute-start(bf16[256,1024]{1,0:T(8,128)(2,1)S(1)} %get-tuple-element.27), channel_id=1, source_target_pairs={{0,1},{1,0},{2,3},{3,2},{4,5},{5,4},{6,7},{7,6},{8,9},{9,8},{10,11... | collective-permute-start | bytes 1572872 | tf_op jit(solution)/shard_map/ppermute | solution.py:21
  22.8 1.5 %collective-permute-start.9 = (bf16[2,1024,128]{2,1,0:T(8,128)(2,1)S(1)}, bf16[2,1024,128]{2,1,0:T(8,128)(2,1)S(1)}, u32[]{:S(2)}, u32[]{:S(2)}) collective-permute-start(bf16[2,1024,128]{2,1,0:T(8,128)(2,1)S(1)} %copy-done), channel_id=1, source_target_pairs={{0,8},{4,12},{8,0},{12,4},{1,9},{5,13},{9,1},{13,5},{2,10},{6,14},... | collective-permute-start | bytes 1572872 | tf_op jit(solution)/shard_map/ppermute | solution.py:21
  24.3 4.0 %projection_rest.1 = (bf16[256,768]{1,0:T(8,128)(2,1)S(1)}, bf16[256,2048]{1,0:T(8,128)(2,1)S(1)}) custom-call(s32[1]{0:T(128)} %bitcast.1.me_ref, bf16[256,1024]{1,0:T(8,128)(2,1)S(1)} %get-tuple-element.25.x_ref.refs_4_, bf16[1024,4096]{1,0:T(8,128)(2,1)} %refs_5_.3), custom_call_target="tpu_custom_call" | custom-call | flops 1 | bytes 1 | tf_op jit(solution)/shard_map/projection_rest/pallas_call | solution.py:238
  28.5 0.5 collective-permute-start.6
  29.0 9.5 %collective-permute-done.3.refs_1_.refs_5_ = bf16[256,1024]{1,0:T(8,128)(2,1)S(1)} collective-permute-done((bf16[256,1024]{1,0:T(8,128)(2,1)S(1)}, bf16[256,1024]{1,0:T(8,128)(2,1)S(1)}, u32[]{:S(2)}, u32[]{:S(2)}) %collective-permute-start.3) | collective-permute-done | bytes 524320 | tf_op jit(solution)/shard_map/ppermute | solution.py:21
  38.6 0.2 collective-permute-start.4
  38.8 0.5 collective-permute-start.10
  39.3 6.6 %collective-permute-done.5.refs_3_.refs_8_ = bf16[256,768]{1,0:T(8,128)(2,1)S(1)} collective-permute-done((bf16[256,768]{1,0:T(8,128)(2,1)S(1)}, bf16[256,768]{1,0:T(8,128)(2,1)S(1)}, u32[]{:S(2)}, u32[]{:S(2)}) %collective-permute-start.5) | collective-permute-done | bytes 393248 | tf_op jit(solution)/shard_map/ppermute | solution.py:21
  46.1 2.2 %projection_last.1 = (bf16[256,384]{1,0:T(8,128)(2,1)S(1)}, f32[256,128]{1,0:T(8,128)S(1)}) custom-call(s32[1]{0:T(128)} %bitcast.1.me_ref, s32[1]{0:T(128)} %bitcast.refs_0_, s32[4]{0:T(128)} %refs_1_.7, s32[8]{0:T(128)} %refs_2_.5, s32[8]{0:T(128)} %refs_3_.5, bf16[256,1024]{1,0:T(8,128)(2,1)S(1)} %get-tuple-element.25.x_ref.refs_4_, ...), custom_call_target="tpu_custom_call" | custom-call | flops 1 | bytes 1 | tf_op jit(solution)/shard_map/projection_last/pallas_call | solution.py:280
  48.2 0.4 collective-permute-start.11
  48.7 4.4 %collective-permute-start.7 = (bf16[256,384]{1,0:T(8,128)(2,1)S(1)}, bf16[256,384]{1,0:T(8,128)(2,1)S(1)}, u32[]{:S(2)}, u32[]{:S(2)}) collective-permute-start(bf16[256,384]{1,0:T(8,128)(2,1)S(1)} %combine.4.refs_10_.refs_0_), channel_id=1, source_target_pairs={{0,2},{1,3},{2,0},{3,1},{4,6},{5,7},{6,4},{7,5},{8,10},{9,11},{10,... | collective-permute-start | bytes 589832 | tf_op jit(solution)/shard_map/ppermute | solution.py:21
  53.1 0.5 collective-permute-start.14
  53.6 3.8 %collective-permute-done.11.refs_3_.refs_11_ = bf16[256,384]{1,0:T(8,128)(2,1)S(1)} collective-permute-done((bf16[256,384]{1,0:T(8,128)(2,1)S(1)}, bf16[256,384]{1,0:T(8,128)(2,1)S(1)}, u32[]{:S(2)}, u32[]{:S(2)}) %collective-permute-start.11) | collective-permute-done | bytes 196640 | tf_op jit(solution)/shard_map/ppermute | solution.py:21
  57.5 1.1 %collective-permute-start.12 = (bf16[256,256]{1,0:T(8,128)(2,1)S(1)}, bf16[256,256]{1,0:T(8,128)(2,1)S(1)}, u32[]{:S(2)}, u32[]{:S(2)}) collective-permute-start(bf16[256,256]{1,0:T(8,128)(2,1)S(1)} %get-tuple-element.35), channel_id=1, source_target_pairs={{0,2},{1,3},{2,0},{3,1},{4,6},{5,7},{6,4},{7,5},{8,10},{9,11},{10,... | collective-permute-start | bytes 393224 | tf_op jit(solution)/shard_map/ppermute | solution.py:21
  58.6 5.4 %collective-permute-done.7.refs_9_ = bf16[256,384]{1,0:T(8,128)(2,1)S(1)} collective-permute-done((bf16[256,384]{1,0:T(8,128)(2,1)S(1)}, bf16[256,384]{1,0:T(8,128)(2,1)S(1)}, u32[]{:S(2)}, u32[]{:S(2)}) %collective-permute-start.7) | collective-permute-done | bytes 196640 | tf_op jit(solution)/shard_map/ppermute | solution.py:21
  63.9 2.0 %collective-permute-done.12.refs_12_.refs_14_ = bf16[256,256]{1,0:T(8,128)(2,1)S(1)} collective-permute-done((bf16[256,256]{1,0:T(8,128)(2,1)S(1)}, bf16[256,256]{1,0:T(8,128)(2,1)S(1)}, u32[]{:S(2)}, u32[]{:S(2)}) %collective-permute-start.12) | collective-permute-done | bytes 131104 | tf_op jit(solution)/shard_map/ppermute | solution.py:21
  65.9 2.7 %finish.1 = bf16[64,4,1024]{2,1,0:T(4,128)(2,1)} custom-call(s32[1]{0:T(128)} %bitcast.refs_0_, s32[4]{0:T(128)} %refs_1_.7, s32[8]{0:T(128)} %refs_2_.5, s32[8]{0:T(128)} %refs_3_.5, bf16[256,2048]{1,0:T(8,128)(2,1)S(1)} %get-tuple-element.26.refs_0_.refs_2_.refs_4_.refs_7_.refs_10_, bf16[256,1024]{1,0:T(8,128)(2,1)S(1)} %collective-permute-done.3.refs_1_.refs_5_, ...), custom_call_target="tpu_custom_call" | custom-call | flops 1 | bytes 1 | tf_op jit(solution)/shard_map/finish/pallas_call | solution.py:404
  (22 shorter events, 0.4 us)
Async XLA Ops:
  4.0 10.2 %collective-permute-start = (bf16[64,1024]{1,0:T(8,128)(2,1)S(1)}, bf16[64,1024]{1,0:T(8,128)(2,1)S(1)}, u32[]{:S(2)}, u32[]{:S(2)}) collective-permute-start(bf16[64,1024]{1,0:T(8,128)(2,1)S(1)} %get-tuple-element.23), channel_id=1, source_target_pairs={{0,1},{1,0},{2,3},{3,2},{4,5},{5,4},{6,7},{7,6},{8,9},{9,8},{10,11... | collective-permute-start | bytes 393224 | tf_op jit(solution)/shard_map/ppermute | solution.py:21
  7.1 12.9 %collective-permute-start.1 = (bf16[64,1024]{1,0:T(8,128)(2,1)S(1)}, bf16[64,1024]{1,0:T(8,128)(2,1)S(1)}, u32[]{:S(2)}, u32[]{:S(2)}) collective-permute-start(bf16[64,1024]{1,0:T(8,128)(2,1)S(1)} %get-tuple-element.24), channel_id=1, source_target_pairs={{0,2},{1,3},{2,0},{3,1},{4,6},{5,7},{6,4},{7,5},{8,10},{9,11},{10,... | collective-permute-start | bytes 393224 | tf_op jit(solution)/shard_map/ppermute | solution.py:21
  9.7 10.3 %collective-permute-start.2 = (bf16[64,1024]{1,0:T(8,128)(2,1)S(1)}, bf16[64,1024]{1,0:T(8,128)(2,1)S(1)}, u32[]{:S(2)}, u32[]{:S(2)}) collective-permute-start(bf16[64,1024]{1,0:T(8,128)(2,1)S(1)} %get-tuple-element.22.refs_2_), channel_id=1, source_target_pairs={{0,3},{1,2},{2,1},{3,0},{4,7},{5,6},{6,5},{7,4},{8,11},{9,10},{10,... | collective-permute-start | bytes 393224 | tf_op jit(solution)/shard_map/ppermute | solution.py:21
  14.1 8.7 %copy-start = (bf16[2,1024,128]{2,1,0:T(8,128)(2,1)S(1)}, bf16[2,1024,128]{2,1,0:T(8,128)(2,1)}, u32[]{:S(2)}) copy-start(bf16[2,1024,128]{2,1,0:T(8,128)(2,1)} %refs_6_) | copy-start | bytes 1572868
  20.8 17.7 %collective-permute-start.3 = (bf16[256,1024]{1,0:T(8,128)(2,1)S(1)}, bf16[256,1024]{1,0:T(8,128)(2,1)S(1)}, u32[]{:S(2)}, u32[]{:S(2)}) collective-permute-start(bf16[256,1024]{1,0:T(8,128)(2,1)S(1)} %get-tuple-element.27), channel_id=1, source_target_pairs={{0,1},{1,0},{2,3},{3,2},{4,5},{5,4},{6,7},{7,6},{8,9},{9,8},{10,11... | collective-permute-start | bytes 1572872 | tf_op jit(solution)/shard_map/ppermute | solution.py:21
  22.8 16.0 %collective-permute-start.9 = (bf16[2,1024,128]{2,1,0:T(8,128)(2,1)S(1)}, bf16[2,1024,128]{2,1,0:T(8,128)(2,1)S(1)}, u32[]{:S(2)}, u32[]{:S(2)}) collective-permute-start(bf16[2,1024,128]{2,1,0:T(8,128)(2,1)S(1)} %copy-done), channel_id=1, source_target_pairs={{0,8},{4,12},{8,0},{12,4},{1,9},{5,13},{9,1},{13,5},{2,10},{6,14},... | collective-permute-start | bytes 1572872 | tf_op jit(solution)/shard_map/ppermute | solution.py:21
  24.3 4.2 %copy-start.1 = (bf16[2,128,1024]{2,1,0:T(8,128)(2,1)S(1)}, bf16[2,128,1024]{2,1,0:T(8,128)(2,1)}, u32[]{:S(2)}) copy-start(bf16[2,128,1024]{2,1,0:T(8,128)(2,1)} %refs_15_) | copy-start | bytes 1572868
  28.3 17.6 %collective-permute-start.5 = (bf16[256,768]{1,0:T(8,128)(2,1)S(1)}, bf16[256,768]{1,0:T(8,128)(2,1)S(1)}, u32[]{:S(2)}, u32[]{:S(2)}) collective-permute-start(bf16[256,768]{1,0:T(8,128)(2,1)S(1)} %get-tuple-element.28), channel_id=1, source_target_pairs={{0,1},{1,0},{2,3},{3,2},{4,5},{5,4},{6,7},{7,6},{8,9},{9,8},{10,11... | collective-permute-start | bytes 1179656 | tf_op jit(solution)/shard_map/ppermute | solution.py:21
  28.5 17.5 %collective-permute-start.6 = (bf16[2,128,1024]{2,1,0:T(8,128)(2,1)S(1)}, bf16[2,128,1024]{2,1,0:T(8,128)(2,1)S(1)}, u32[]{:S(2)}, u32[]{:S(2)}) collective-permute-start(bf16[2,128,1024]{2,1,0:T(8,128)(2,1)S(1)} %copy-done.1), channel_id=1, source_target_pairs={{0,8},{4,12},{8,0},{12,4},{1,9},{5,13},{9,1},{13,5},{2,10},{6,14},... | collective-permute-start | bytes 1572872 | tf_op jit(solution)/shard_map/ppermute | solution.py:21
  38.6 15.0 %collective-permute-start.4 = (bf16[256,512]{1,0:T(8,128)(2,1)S(1)}, bf16[256,512]{1,0:T(8,128)(2,1)S(1)}, u32[]{:S(2)}, u32[]{:S(2)}) collective-permute-start(bf16[256,512]{1,0:T(8,128)(2,1)S(1)} %combine.3.refs_0_), channel_id=1, source_target_pairs={{0,2},{1,3},{2,0},{3,1},{4,6},{5,7},{6,4},{7,5},{8,10},{9,11},{10,... | collective-permute-start | bytes 786440 | tf_op jit(solution)/shard_map/ppermute | solution.py:21
  38.8 7.2 %collective-permute-start.8 = (bf16[2,1024,128]{2,1,0:T(8,128)(2,1)S(1)}, bf16[2,1024,128]{2,1,0:T(8,128)(2,1)S(1)}, u32[]{:S(2)}, u32[]{:S(2)}) collective-permute-start(bf16[2,1024,128]{2,1,0:T(8,128)(2,1)S(1)} %copy-done), channel_id=1, source_target_pairs={{0,4},{4,0},{8,12},{12,8},{1,5},{5,1},{9,13},{13,9},{2,6},{6,2},{1... | collective-permute-start | bytes 1572872 | tf_op jit(solution)/shard_map/ppermute | solution.py:21
  38.8 7.2 %collective-permute-start.10 = (bf16[2,1024,128]{2,1,0:T(8,128)(2,1)S(1)}, bf16[2,1024,128]{2,1,0:T(8,128)(2,1)S(1)}, u32[]{:S(2)}, u32[]{:S(2)}) collective-permute-start(bf16[2,1024,128]{2,1,0:T(8,128)(2,1)S(1)} %collective-permute-done.9.refs_8_), channel_id=1, source_target_pairs={{0,4},{4,0},{8,12},{12,8},{1,5},{5,1},{9,13},{13,9},{2,6},{6,2},{1... | collective-permute-start | bytes 1572872 | tf_op jit(solution)/shard_map/ppermute | solution.py:21
  46.0 7.0 %copy-start.2 = (bf16[2,128,1024]{2,1,0:T(8,128)(2,1)S(1)}, bf16[2,128,1024]{2,1,0:T(8,128)(2,1)}, u32[]{:S(2)}) copy-start(bf16[2,128,1024]{2,1,0:T(8,128)(2,1)} %refs_15_) | copy-start | bytes 1572868
  48.2 9.2 %collective-permute-start.11 = (bf16[256,384]{1,0:T(8,128)(2,1)S(1)}, bf16[256,384]{1,0:T(8,128)(2,1)S(1)}, u32[]{:S(2)}, u32[]{:S(2)}) collective-permute-start(bf16[256,384]{1,0:T(8,128)(2,1)S(1)} %get-tuple-element.33), channel_id=1, source_target_pairs={{0,1},{1,0},{2,3},{3,2},{4,5},{5,4},{6,7},{7,6},{8,9},{9,8},{10,11... | collective-permute-start | bytes 589832 | tf_op jit(solution)/shard_map/ppermute | solution.py:21
  48.7 15.2 %collective-permute-start.7 = (bf16[256,384]{1,0:T(8,128)(2,1)S(1)}, bf16[256,384]{1,0:T(8,128)(2,1)S(1)}, u32[]{:S(2)}, u32[]{:S(2)}) collective-permute-start(bf16[256,384]{1,0:T(8,128)(2,1)S(1)} %combine.4.refs_10_.refs_0_), channel_id=1, source_target_pairs={{0,2},{1,3},{2,0},{3,1},{4,6},{5,7},{6,4},{7,5},{8,10},{9,11},{10,... | collective-permute-start | bytes 589832 | tf_op jit(solution)/shard_map/ppermute | solution.py:21
  53.1 10.9 %collective-permute-start.13 = (bf16[2,128,1024]{2,1,0:T(8,128)(2,1)S(1)}, bf16[2,128,1024]{2,1,0:T(8,128)(2,1)S(1)}, u32[]{:S(2)}, u32[]{:S(2)}) collective-permute-start(bf16[2,128,1024]{2,1,0:T(8,128)(2,1)S(1)} %copy-done.2), channel_id=1, source_target_pairs={{0,4},{4,0},{8,12},{12,8},{1,5},{5,1},{9,13},{13,9},{2,6},{6,2},{1... | collective-permute-start | bytes 1572872 | tf_op jit(solution)/shard_map/ppermute | solution.py:21
  53.1 10.9 %collective-permute-start.14 = (bf16[2,128,1024]{2,1,0:T(8,128)(2,1)S(1)}, bf16[2,128,1024]{2,1,0:T(8,128)(2,1)S(1)}, u32[]{:S(2)}, u32[]{:S(2)}) collective-permute-start(bf16[2,128,1024]{2,1,0:T(8,128)(2,1)S(1)} %collective-permute-done.6.refs_1_.refs_17_), channel_id=1, source_target_pairs={{0,4},{4,0},{8,12},{12,8},{1,5},{5,1},{9,13},{13,9},{2,6},{6,2},{1... | collective-permute-start | bytes 1572872 | tf_op jit(solution)/shard_map/ppermute | solution.py:21
  57.5 8.5 %collective-permute-start.12 = (bf16[256,256]{1,0:T(8,128)(2,1)S(1)}, bf16[256,256]{1,0:T(8,128)(2,1)S(1)}, u32[]{:S(2)}, u32[]{:S(2)}) collective-permute-start(bf16[256,256]{1,0:T(8,128)(2,1)S(1)} %get-tuple-element.35), channel_id=1, source_target_pairs={{0,2},{1,3},{2,0},{3,1},{4,6},{5,7},{6,4},{7,5},{8,10},{9,11},{10,... | collective-permute-start | bytes 393224 | tf_op jit(solution)/shard_map/ppermute | solution.py:21

commit v2 on v1

--- a/solution.py
+++ b/solution.py
@@ -14,6 +14,7 @@
 bf16 = jnp.bfloat16
 hint = pl.CostEstimate(flops=1, bytes_accessed=1, transcendentals=0)
 long = pl.CostEstimate(flops=10**11, bytes_accessed=10**9, transcendentals=0)
+mid = pl.CostEstimate(flops=8 * 10**9, bytes_accessed=8 * 10**6, transcendentals=0)
 
 
 def swap(x, axis, bit):
@@ -183,29 +184,49 @@
     return (slot // held) ^ rep_ref[0], slot % held, rank_ref[adapter]
 
 
-def project_kernel(me_ref, *refs):
-    *pieces, w_ref, out_ref, x_ref = refs
+def gather_kernel(me_ref, *refs, places):
+    *pieces, x_ref = refs
     rows = pieces[0].shape[0]
-    for p, piece in enumerate(pieces):
+    for p, piece in zip(places, pieces):
         x_ref[pl.ds(pl.multiple_of((me_ref[0] ^ p) * rows, rows), rows), :] = piece[...]
-    out_ref[...] = jnp.dot(x_ref[...], w_ref[...], preferred_element_type=f32).astype(bf16)
-
-
-def project(pieces, weight, me):
-    total = sum(x.shape[0] for x in pieces)
-    return pl.pallas_call(
-        project_kernel,
-        in_specs=[pl.BlockSpec(memory_space=pltpu.SMEM)]
-        + [pl.BlockSpec(memory_space=pltpu.VMEM)] * (len(pieces) + 1),
-        out_specs=[pl.BlockSpec(memory_space=pltpu.VMEM)] * 2,
-        out_shape=[
-            jax.ShapeDtypeStruct((total, weight.shape[1]), bf16),
-            jax.ShapeDtypeStruct((total, pieces[0].shape[1]), bf16),
-        ],
+
+
+def gather(pieces, n_tp, me):
+    places = list(pieces)
+    rows, feats = pieces[places[0]].shape
+    vmem = pl.BlockSpec(memory_space=pltpu.VMEM)
+    return pl.pallas_call(
+        functools.partial(gather_kernel, places=places),
+        in_specs=[pl.BlockSpec(memory_space=pltpu.SMEM)] + [vmem] * len(places),
+        out_specs=vmem,
+        out_shape=jax.ShapeDtypeStruct((rows * n_tp, feats), bf16),
         compiler_params=pltpu.CompilerParams(vmem_limit_bytes=8 << 20),
         cost_estimate=long,
+        name="gather",
+    )(me, *(pieces[p] for p in places))
+
+
+def project_kernel(me_ref, piece_ref, w_ref, _, out_ref, x_ref, *, place):
+    rows = piece_ref.shape[0]
+    x_ref[pl.ds(pl.multiple_of((me_ref[0] ^ place) * rows, rows), rows), :] = piece_ref[...]
+    out_ref[...] = jnp.dot(x_ref[...], w_ref[...], preferred_element_type=f32).astype(bf16)
+
+
+def project(x, piece, place, weight, me):
+    vmem = pl.BlockSpec(memory_space=pltpu.VMEM)
+    return pl.pallas_call(
+        functools.partial(project_kernel, place=place),
+        in_specs=[pl.BlockSpec(memory_space=pltpu.SMEM)] + [vmem] * 3,
+        out_specs=[vmem] * 2,
+        out_shape=[
+            jax.ShapeDtypeStruct((x.shape[0], weight.shape[1]), bf16),
+            jax.ShapeDtypeStruct(x.shape, bf16),
+        ],
+        input_output_aliases={3: 1},
+        compiler_params=pltpu.CompilerParams(vmem_limit_bytes=12 << 20),
+        cost_estimate=long,
         name="projection",
-    )(me, *pieces, in_vmem(weight))
+    )(me, piece, in_vmem(weight), x)
 
 
 def project_rest_kernel(me_ref, x_ref, w_ref, *refs, order, widths, columns):
@@ -322,7 +343,7 @@
     send_ref[:, :wide] = total.astype(bf16)
 
 
-def combine(addends, wide, low, waits):
+def combine(addends, wide, low, waits, cost):
     arrays = [a for a, _ in addends]
     rows = arrays[0].shape[0]
     rank = 0 if low is None else low.shape[1]
@@ -343,7 +364,7 @@
         out_specs=[pl.BlockSpec(memory_space=pltpu.VMEM)] * len(out_shape),
         out_shape=out_shape,
         compiler_params=pltpu.CompilerParams(vmem_limit_bytes=8 << 20),
-        cost_estimate=long,
+        cost_estimate=cost,
         name="combine",
     )(*waits, *arrays)
 
@@ -485,22 +506,44 @@
             bit //= 2
         return [held[p] for p in range(n_rep)]
 
-    far, near = range(1, n_tp), range(1)
+    far, near = range(2, n_tp), range(2)
     own = dict(zip(far, attend(*arrays, me, far, n_tp)))
-    pieces = {p: swap(own[p], "tp", p) for p in reversed(far)}
+    pieces = {p: swap(own[p], "tp", p) for p in far}
     own.update(zip(near, attend(*arrays, me, near, n_tp, [own[n_tp - 1]])))
-    pieces[0] = own[0]
-    down_across = swap(after(adapter_down_weight, own[0]), "rep", top_bit)
+    piece = swap(own[1], "tp", 1)
     weight = load(output_projection_weight, me, order[:owners], widths[0], columns, [own[0]])
-
-    send, x = project([pieces[p] for p in range(n_tp)], weight, me)
+    down_across = swap(after(adapter_down_weight, weight), "rep", top_bit)
+
+    send, x = project(gather({0: own[0], **pieces}, n_tp, me), piece, 1, weight, me)
     *sends, keep = project_rest(x, output_projection_weight, me, order, widths, columns)
+    downs = relay(adapter_down_weight, down_across, keep)
     up_across = swap(after(adapter_up_weight, keep), "rep", top_bit)
     gots = [swap(send, "tp", 1) for send in (send, *sends)]
     finals, last = [], []
-    low = None
     for q in range(parts):
-        if q == parts - 1:
+        addends = [(keep, owners * starts[q]), (gots[q], 0)]
+        wide = owners * widths[q]
+        bit = 2
+        while bit < n_tp:
+            wide //= 2
+            first = bit == 2
+            waits = last + ([up_across] if q == 1 else []) + ([finals[q - 2][-1][0]] if q >= 2 else [])
+            out = combine(
+                addends,
+                wide,
+                low if q == parts - 1 else None,
+                waits if first else [],
+                (long if q else mid) if first else hint,
+            )
+            if first:
+                last = [out[0]]
+            if q == parts - 1:
+                low = out[1]
+            got = swap(out[0], "tp", bit)
+            addends = [(a, off + wide) for a, off in addends] + [(got, 0)]
+            bit *= 2
+        finals.append(addends)
+        if q == 0:
             send, low = project_last(
                 x,
                 output_projection_weight,
@@ -508,30 +551,12 @@
                 me,
                 table,
                 order[:owners],
-                widths[q],
+                widths[-1],
                 columns,
                 per_block,
                 last,
             )
             gots.append(swap(send, "tp", 1))
-        addends = [(keep, owners * starts[q]), (gots[q], 0)]
-        wide = owners * widths[q]
-        bit = 2
-        while bit < n_tp:
-            wide //= 2
-            first = bit == 2
-            waits = last + ([up_across] if q == 1 else []) + ([finals[q - 2][-1][0]] if q >= 2 else [])
-            out = combine(addends, wide, low, waits if first else [])
-            if first:
-                last = [out[0]]
-            if low is not None:
-                low = out[1]
-            got = swap(out[0], "tp", bit)
-            addends = [(a, off + wide) for a, off in addends] + [(got, 0)]
-            bit *= 2
-        finals.append(addends)
-        if q == 0:
-            downs = relay(adapter_down_weight, down_across, last[0])
         if q == 1:
             ups = relay(adapter_up_weight, up_across, last[0])
     return finish(finals, widths, 0, low, got, ups, table, None, steps, columns, per_block)

time: 68.9 us -> 67.3 us (0.977)
  starting transfers between devices: 17 us -> 15.6 us
  waiting for transfers between devices: 33.2 us -> 32.5 us
    ppermute x15, starting transfers between devices: 17 us -> 15.6 us  [swap(): return lax.ppermute(x, axis, [(i, i ^ bit) for i in range(n)])]
    ppermute x15, waiting for transfers between devices: 33.2 us -> 32.5 us  [swap(): return lax.ppermute(x, axis, [(i, i ^ bit) for i in range(n)])]
  transfers between devices with their start and end apart: 15 -> 15, of which waited for: 7 -> 8; matrix products, arithmetic and copies ran while one was open for 0% -> 0% of each run, Pallas kernels for 16% -> 19%
where the time goes in v2:
time: 67.3 us; the launch traced here: 67 us
  waiting for transfers between devices  32.5 us (48%)
  Pallas kernels  18.7 us (28%)
  starting transfers between devices  15.6 us (23%)
    ppermute x15, waiting for transfers between devices, swap(): return lax.ppermute(x, axis, [(i, i ^ bit) for i in range(n)])  32.5 us
    ppermute x15, starting transfers between devices, swap(): return lax.ppermute(x, axis, [(i, i ^ bit) for i in range(n)])  15.6 us
    pallas_call x2, Pallas kernels, attend(): pl.pallas_call(functools.partial(attend_kernel, pieces=pieces, n_tp=n_tp,...  6.94 us
    pallas_call x1, Pallas kernels, project_rest(): pl.pallas_call(functools.partial(project_rest_kernel, order=order, widths...  4.02 us
    pallas_call x1, Pallas kernels, finish(): pl.pallas_call(functools.partial(finish_kernel, offsets=[[off for _, off...  2.75 us
    pallas_call x1, Pallas kernels, project_last(): pl.pallas_call(functools.partial(project_last_kernel, owners=owners, widt...  2.58 us
    pallas_call x1, Pallas kernels, load(): pl.pallas_call(functools.partial(load_kernel, owners=owners, part=part, c...  1.56 us
  transfers between devices with their start and end apart: 15, of which 8 were waited for; matrix products, arithmetic and copies ran while one was open for 0% of the time, Pallas kernels for 19%

profile of v2, /device:TPU:0, one launch (start us, length us, event | category | flops | bytes accessed | tf_op | source)
XLA Modules:
  0.0 67.0 jit_solution(16572824656668226839)
XLA Ops:
  0.0 3.5 %attention.2 = (bf16[64,1024]{1,0:T(8,128)(2,1)S(1)}, bf16[64,1024]{1,0:T(8,128)(2,1)S(1)}) custom-call(s32[1]{0:T(128)} %bitcast.1.me_ref, s32[16]{0:T(128)} %len_ref.3, bf16[16,4,4096]{2,1,0:T(4,128)(2,1)} %q_ref.3, bf16[16,4,4,128]{3,2,1,0:T(4,128)(2,1)} %dk_ref.3, bf16[16,4,4,128]{3,2,1,0:T(4,128)(2,1)} %dv_ref.3, bf16[16,4,128,128]{3,2,1,0:T(8,128)(2,1)} %refs_1_.5, ...), custom_call_target="tpu_custom_call" | custom-call | flops 1 | bytes 1 | tf_op jit(solution)/shard_map/attention/pallas_call | solution.py:124
  3.5 5.1 %collective-permute-start.2 = (bf16[64,1024]{1,0:T(8,128)(2,1)S(1)}, bf16[64,1024]{1,0:T(8,128)(2,1)S(1)}, u32[]{:S(2)}, u32[]{:S(2)}) collective-permute-start(bf16[64,1024]{1,0:T(8,128)(2,1)S(1)} %get-tuple-element.23.refs_4_), channel_id=1, source_target_pairs={{0,3},{1,2},{2,1},{3,0},{4,7},{5,6},{6,5},{7,4},{8,11},{9,10},{10,... | collective-permute-start | bytes 393224 | tf_op jit(solution)/shard_map/ppermute | solution.py:22
  8.6 3.5 %attention.3 = (bf16[64,1024]{1,0:T(8,128)(2,1)S(1)}, bf16[64,1024]{1,0:T(8,128)(2,1)S(1)}) custom-call(s32[1]{0:T(128)} %bitcast.1.me_ref, s32[16]{0:T(128)} %len_ref.3, bf16[16,4,4096]{2,1,0:T(4,128)(2,1)} %q_ref.3, bf16[16,4,4,128]{3,2,1,0:T(4,128)(2,1)} %dk_ref.3, bf16[16,4,4,128]{3,2,1,0:T(4,128)(2,1)} %dv_ref.3, bf16[16,4,128,128]{3,2,1,0:T(8,128)(2,1)} %refs_1_.5, ...), custom_call_target="tpu_custom_call" | custom-call | flops 1 | bytes 1 | tf_op jit(solution)/shard_map/attention/pallas_call | solution.py:124
  12.1 0.7 %collective-permute-start = (bf16[64,1024]{1,0:T(8,128)(2,1)S(1)}, bf16[64,1024]{1,0:T(8,128)(2,1)S(1)}, u32[]{:S(2)}, u32[]{:S(2)}) collective-permute-start(bf16[64,1024]{1,0:T(8,128)(2,1)S(1)} %get-tuple-element.24), channel_id=1, source_target_pairs={{0,1},{1,0},{2,3},{3,2},{4,5},{5,4},{6,7},{7,6},{8,9},{9,8},{10,11... | collective-permute-start | bytes 393224 | tf_op jit(solution)/shard_map/ppermute | solution.py:22
  12.8 1.6 %load.1.w_ref = bf16[1024,1024]{1,0:T(8,128)(2,1)S(1)} custom-call(s32[1]{0:T(128)} %bitcast.1.me_ref, bf16[1024,4096]{1,0:T(8,128)(2,1)} %refs_5_.1, bf16[64,1024]{1,0:T(8,128)(2,1)S(1)} %get-tuple-element.25.refs_0_), custom_call_target="tpu_custom_call" | custom-call | flops 1 | bytes 1 | tf_op jit(solution)/shard_map/load/pallas_call | solution.py:167
  14.3 1.7 %collective-permute-start.9 = (bf16[2,1024,128]{2,1,0:T(8,128)(2,1)}, bf16[2,1024,128]{2,1,0:T(8,128)(2,1)}, u32[]{:S(2)}, u32[]{:S(2)}) collective-permute-start(bf16[2,1024,128]{2,1,0:T(8,128)(2,1)} %refs_6_), channel_id=1, source_target_pairs={{0,8},{4,12},{8,0},{12,4},{1,9},{5,13},{9,1},{13,5},{2,10},{6,14},... | collective-permute-start | bytes 1572872 | tf_op jit(solution)/shard_map/ppermute | solution.py:22
  16.1 3.7 %collective-permute-done.1.refs_1_ = bf16[64,1024]{1,0:T(8,128)(2,1)S(1)} collective-permute-done((bf16[64,1024]{1,0:T(8,128)(2,1)S(1)}, bf16[64,1024]{1,0:T(8,128)(2,1)S(1)}, u32[]{:S(2)}, u32[]{:S(2)}) %collective-permute-start.1) | collective-permute-done | bytes 131104 | tf_op jit(solution)/shard_map/ppermute | solution.py:22
  19.8 0.1 collective-permute-done.piece_ref
  19.9 0.7 %projection.1 = (bf16[256,1024]{1,0:T(8,128)(2,1)S(1)}, bf16[256,1024]{1,0:T(8,128)(2,1)S(1)}) custom-call(s32[1]{0:T(128)} %bitcast.1.me_ref, bf16[64,1024]{1,0:T(8,128)(2,1)S(1)} %collective-permute-done.piece_ref, bf16[1024,1024]{1,0:T(8,128)(2,1)S(1)} %load.1.w_ref, bf16[256,1024]{1,0:T(8,128)(2,1)S(1)} %gather.1._), custom_call_target="tpu_custom_call", output_to_operand_aliasing={{1}: (3, {})} | custom-call | flops 99999997952 | bytes 1000000000 | tf_op jit(solution)/shard_map/projection/pallas_call | solution.py:217
  20.6 0.1 collective-permute-start.3
  20.7 4.0 %projection_rest.1 = (bf16[256,768]{1,0:T(8,128)(2,1)S(1)}, bf16[256,2048]{1,0:T(8,128)(2,1)S(1)}) custom-call(s32[1]{0:T(128)} %bitcast.1.me_ref, bf16[256,1024]{1,0:T(8,128)(2,1)S(1)} %get-tuple-element.27.x_ref.refs_4_, bf16[1024,4096]{1,0:T(8,128)(2,1)} %refs_5_.1), custom_call_target="tpu_custom_call" | custom-call | flops 1 | bytes 1 | tf_op jit(solution)/shard_map/projection_rest/pallas_call | solution.py:259
  24.8 1.6 %collective-permute-start.6 = (bf16[2,128,1024]{2,1,0:T(8,128)(2,1)S(1)}, bf16[2,128,1024]{2,1,0:T(8,128)(2,1)S(1)}, u32[]{:S(2)}, u32[]{:S(2)}) collective-permute-start(bf16[2,128,1024]{2,1,0:T(8,128)(2,1)S(1)} %copy-done), channel_id=1, source_target_pairs={{0,8},{4,12},{8,0},{12,4},{1,9},{5,13},{9,1},{13,5},{2,10},{6,14},... | collective-permute-start | bytes 1572872 | tf_op jit(solution)/shard_map/ppermute | solution.py:22
  26.3 2.0 %collective-permute-start.5 = (bf16[256,768]{1,0:T(8,128)(2,1)S(1)}, bf16[256,768]{1,0:T(8,128)(2,1)S(1)}, u32[]{:S(2)}, u32[]{:S(2)}) collective-permute-start(bf16[256,768]{1,0:T(8,128)(2,1)S(1)} %get-tuple-element.30), channel_id=1, source_target_pairs={{0,1},{1,0},{2,3},{3,2},{4,5},{5,4},{6,7},{7,6},{8,9},{9,8},{10,11... | collective-permute-start | bytes 1179656 | tf_op jit(solution)/shard_map/ppermute | solution.py:22
  28.3 0.8 %collective-permute-done.9.refs_8_ = bf16[2,1024,128]{2,1,0:T(8,128)(2,1)} collective-permute-done((bf16[2,1024,128]{2,1,0:T(8,128)(2,1)}, bf16[2,1024,128]{2,1,0:T(8,128)(2,1)}, u32[]{:S(2)}, u32[]{:S(2)}) %collective-permute-start.9) | collective-permute-done | bytes 524320 | tf_op jit(solution)/shard_map/ppermute | solution.py:22
  29.1 9.3 %collective-permute-done.3.refs_1_.refs_5_ = bf16[256,1024]{1,0:T(8,128)(2,1)S(1)} collective-permute-done((bf16[256,1024]{1,0:T(8,128)(2,1)S(1)}, bf16[256,1024]{1,0:T(8,128)(2,1)S(1)}, u32[]{:S(2)}, u32[]{:S(2)}) %collective-permute-start.3) | collective-permute-done | bytes 524320 | tf_op jit(solution)/shard_map/ppermute | solution.py:22
  38.5 2.6 %projection_last.1 = (bf16[256,384]{1,0:T(8,128)(2,1)S(1)}, f32[256,128]{1,0:T(8,128)S(1)}) custom-call(s32[1]{0:T(128)} %bitcast.1.me_ref, s32[1]{0:T(128)} %bitcast.refs_0_, s32[4]{0:T(128)} %refs_1_.7, s32[8]{0:T(128)} %refs_2_.7, s32[8]{0:T(128)} %refs_3_.7, bf16[256,1024]{1,0:T(8,128)(2,1)S(1)} %get-tuple-element.27.x_ref.refs_4_, ...), custom_call_target="tpu_custom_call" | custom-call | flops 1 | bytes 1 | tf_op jit(solution)/shard_map/projection_last/pallas_call | solution.py:301
  41.1 2.9 %collective-permute-start.11 = (bf16[256,384]{1,0:T(8,128)(2,1)S(1)}, bf16[256,384]{1,0:T(8,128)(2,1)S(1)}, u32[]{:S(2)}, u32[]{:S(2)}) collective-permute-start(bf16[256,384]{1,0:T(8,128)(2,1)S(1)} %get-tuple-element.35), channel_id=1, source_target_pairs={{0,1},{1,0},{2,3},{3,2},{4,5},{5,4},{6,7},{7,6},{8,9},{9,8},{10,11... | collective-permute-start | bytes 589832 | tf_op jit(solution)/shard_map/ppermute | solution.py:22
  44.0 4.7 %collective-permute-done.5.refs_3_.refs_8_ = bf16[256,768]{1,0:T(8,128)(2,1)S(1)} collective-permute-done((bf16[256,768]{1,0:T(8,128)(2,1)S(1)}, bf16[256,768]{1,0:T(8,128)(2,1)S(1)}, u32[]{:S(2)}, u32[]{:S(2)}) %collective-permute-start.5) | collective-permute-done | bytes 393248 | tf_op jit(solution)/shard_map/ppermute | solution.py:22
  48.9 0.5 collective-permute-start.13
  49.4 4.5 %collective-permute-done.4.refs_1_.refs_6_ = bf16[256,512]{1,0:T(8,128)(2,1)S(1)} collective-permute-done((bf16[256,512]{1,0:T(8,128)(2,1)S(1)}, bf16[256,512]{1,0:T(8,128)(2,1)S(1)}, u32[]{:S(2)}, u32[]{:S(2)}) %collective-permute-start.4) | collective-permute-done | bytes 262176 | tf_op jit(solution)/shard_map/ppermute | solution.py:22
  54.0 0.9 %collective-permute-start.12 = (bf16[256,256]{1,0:T(8,128)(2,1)S(1)}, bf16[256,256]{1,0:T(8,128)(2,1)S(1)}, u32[]{:S(2)}, u32[]{:S(2)}) collective-permute-start(bf16[256,256]{1,0:T(8,128)(2,1)S(1)} %get-tuple-element.37), channel_id=1, source_target_pairs={{0,2},{1,3},{2,0},{3,1},{4,6},{5,7},{6,4},{7,5},{8,10},{9,11},{10,... | collective-permute-start | bytes 393224 | tf_op jit(solution)/shard_map/ppermute | solution.py:22
  54.8 6.6 %collective-permute-done.7.refs_9_ = bf16[256,384]{1,0:T(8,128)(2,1)S(1)} collective-permute-done((bf16[256,384]{1,0:T(8,128)(2,1)S(1)}, bf16[256,384]{1,0:T(8,128)(2,1)S(1)}, u32[]{:S(2)}, u32[]{:S(2)}) %collective-permute-start.7) | collective-permute-done | bytes 196640 | tf_op jit(solution)/shard_map/ppermute | solution.py:22
  61.5 2.8 %collective-permute-done.12.refs_12_.refs_14_ = bf16[256,256]{1,0:T(8,128)(2,1)S(1)} collective-permute-done((bf16[256,256]{1,0:T(8,128)(2,1)S(1)}, bf16[256,256]{1,0:T(8,128)(2,1)S(1)}, u32[]{:S(2)}, u32[]{:S(2)}) %collective-permute-start.12) | collective-permute-done | bytes 131104 | tf_op jit(solution)/shard_map/ppermute | solution.py:22
  64.3 2.7 %finish.1 = bf16[64,4,1024]{2,1,0:T(4,128)(2,1)} custom-call(s32[1]{0:T(128)} %bitcast.refs_0_, s32[4]{0:T(128)} %refs_1_.7, s32[8]{0:T(128)} %refs_2_.7, s32[8]{0:T(128)} %refs_3_.7, bf16[256,2048]{1,0:T(8,128)(2,1)S(1)} %get-tuple-element.28.refs_0_.refs_2_.refs_4_.refs_7_.refs_10_, bf16[256,1024]{1,0:T(8,128)(2,1)S(1)} %collective-permute-done.3.refs_1_.refs_5_, ...), custom_call_target="tpu_custom_call" | custom-call | flops 1 | bytes 1 | tf_op jit(solution)/shard_map/finish/pallas_call | solution.py:425
  (19 shorter events, 0.4 us)
Async XLA Ops:
  3.5 12.6 %collective-permute-start.2 = (bf16[64,1024]{1,0:T(8,128)(2,1)S(1)}, bf16[64,1024]{1,0:T(8,128)(2,1)S(1)}, u32[]{:S(2)}, u32[]{:S(2)}) collective-permute-start(bf16[64,1024]{1,0:T(8,128)(2,1)S(1)} %get-tuple-element.23.refs_4_), channel_id=1, source_target_pairs={{0,3},{1,2},{2,1},{3,0},{4,7},{5,6},{6,5},{7,4},{8,11},{9,10},{10,... | collective-permute-start | bytes 393224 | tf_op jit(solution)/shard_map/ppermute | solution.py:22
  8.6 11.2 %collective-permute-start.1 = (bf16[64,1024]{1,0:T(8,128)(2,1)S(1)}, bf16[64,1024]{1,0:T(8,128)(2,1)S(1)}, u32[]{:S(2)}, u32[]{:S(2)}) collective-permute-start(bf16[64,1024]{1,0:T(8,128)(2,1)S(1)} %get-tuple-element.26), channel_id=1, source_target_pairs={{0,2},{1,3},{2,0},{3,1},{4,6},{5,7},{6,4},{7,5},{8,10},{9,11},{10,... | collective-permute-start | bytes 393224 | tf_op jit(solution)/shard_map/ppermute | solution.py:22
  12.1 7.8 %collective-permute-start = (bf16[64,1024]{1,0:T(8,128)(2,1)S(1)}, bf16[64,1024]{1,0:T(8,128)(2,1)S(1)}, u32[]{:S(2)}, u32[]{:S(2)}) collective-permute-start(bf16[64,1024]{1,0:T(8,128)(2,1)S(1)} %get-tuple-element.24), channel_id=1, source_target_pairs={{0,1},{1,0},{2,3},{3,2},{4,5},{5,4},{6,7},{7,6},{8,9},{9,8},{10,11... | collective-permute-start | bytes 393224 | tf_op jit(solution)/shard_map/ppermute | solution.py:22
  14.3 14.8 %collective-permute-start.9 = (bf16[2,1024,128]{2,1,0:T(8,128)(2,1)}, bf16[2,1024,128]{2,1,0:T(8,128)(2,1)}, u32[]{:S(2)}, u32[]{:S(2)}) collective-permute-start(bf16[2,1024,128]{2,1,0:T(8,128)(2,1)} %refs_6_), channel_id=1, source_target_pairs={{0,8},{4,12},{8,0},{12,4},{1,9},{5,13},{9,1},{13,5},{2,10},{6,14},... | collective-permute-start | bytes 1572872 | tf_op jit(solution)/shard_map/ppermute | solution.py:22
  20.6 17.7 %collective-permute-start.3 = (bf16[256,1024]{1,0:T(8,128)(2,1)S(1)}, bf16[256,1024]{1,0:T(8,128)(2,1)S(1)}, u32[]{:S(2)}, u32[]{:S(2)}) collective-permute-start(bf16[256,1024]{1,0:T(8,128)(2,1)S(1)} %get-tuple-element.29), channel_id=1, source_target_pairs={{0,1},{1,0},{2,3},{3,2},{4,5},{5,4},{6,7},{7,6},{8,9},{9,8},{10,11... | collective-permute-start | bytes 1572872 | tf_op jit(solution)/shard_map/ppermute | solution.py:22
  20.7 4.0 %copy-start = (bf16[2,128,1024]{2,1,0:T(8,128)(2,1)S(1)}, bf16[2,128,1024]{2,1,0:T(8,128)(2,1)}, u32[]{:S(2)}) copy-start(bf16[2,128,1024]{2,1,0:T(8,128)(2,1)} %refs_15_) | copy-start | bytes 1572868
  24.8 23.9 %collective-permute-start.6 = (bf16[2,128,1024]{2,1,0:T(8,128)(2,1)S(1)}, bf16[2,128,1024]{2,1,0:T(8,128)(2,1)S(1)}, u32[]{:S(2)}, u32[]{:S(2)}) collective-permute-start(bf16[2,128,1024]{2,1,0:T(8,128)(2,1)S(1)} %copy-done), channel_id=1, source_target_pairs={{0,8},{4,12},{8,0},{12,4},{1,9},{5,13},{9,1},{13,5},{2,10},{6,14},... | collective-permute-start | bytes 1572872 | tf_op jit(solution)/shard_map/ppermute | solution.py:22
  26.3 22.4 %collective-permute-start.5 = (bf16[256,768]{1,0:T(8,128)(2,1)S(1)}, bf16[256,768]{1,0:T(8,128)(2,1)S(1)}, u32[]{:S(2)}, u32[]{:S(2)}) collective-permute-start(bf16[256,768]{1,0:T(8,128)(2,1)S(1)} %get-tuple-element.30), channel_id=1, source_target_pairs={{0,1},{1,0},{2,3},{3,2},{4,5},{5,4},{6,7},{7,6},{8,9},{9,8},{10,11... | collective-permute-start | bytes 1179656 | tf_op jit(solution)/shard_map/ppermute | solution.py:22
  28.3 10.2 %collective-permute-start.8 = (bf16[2,1024,128]{2,1,0:T(8,128)(2,1)}, bf16[2,1024,128]{2,1,0:T(8,128)(2,1)S(1)}, u32[]{:S(2)}, u32[]{:S(2)}) collective-permute-start(bf16[2,1024,128]{2,1,0:T(8,128)(2,1)} %refs_6_), channel_id=1, source_target_pairs={{0,4},{4,0},{8,12},{12,8},{1,5},{5,1},{9,13},{13,9},{2,6},{6,2},{1... | collective-permute-start | bytes 1572872 | tf_op jit(solution)/shard_map/ppermute | solution.py:22
  29.1 9.4 %collective-permute-start.10 = (bf16[2,1024,128]{2,1,0:T(8,128)(2,1)}, bf16[2,1024,128]{2,1,0:T(8,128)(2,1)S(1)}, u32[]{:S(2)}, u32[]{:S(2)}) collective-permute-start(bf16[2,1024,128]{2,1,0:T(8,128)(2,1)} %collective-permute-done.9.refs_8_), channel_id=1, source_target_pairs={{0,4},{4,0},{8,12},{12,8},{1,5},{5,1},{9,13},{13,9},{2,6},{6,2},{1... | collective-permute-start | bytes 1572872 | tf_op jit(solution)/shard_map/ppermute | solution.py:22
  38.4 15.5 %collective-permute-start.4 = (bf16[256,512]{1,0:T(8,128)(2,1)S(1)}, bf16[256,512]{1,0:T(8,128)(2,1)S(1)}, u32[]{:S(2)}, u32[]{:S(2)}) collective-permute-start(bf16[256,512]{1,0:T(8,128)(2,1)S(1)} %combine.3.refs_0_.refs_10_), channel_id=1, source_target_pairs={{0,2},{1,3},{2,0},{3,1},{4,6},{5,7},{6,4},{7,5},{8,10},{9,11},{10,... | collective-permute-start | bytes 786440 | tf_op jit(solution)/shard_map/ppermute | solution.py:22
  41.1 12.8 %collective-permute-start.11 = (bf16[256,384]{1,0:T(8,128)(2,1)S(1)}, bf16[256,384]{1,0:T(8,128)(2,1)S(1)}, u32[]{:S(2)}, u32[]{:S(2)}) collective-permute-start(bf16[256,384]{1,0:T(8,128)(2,1)S(1)} %get-tuple-element.35), channel_id=1, source_target_pairs={{0,1},{1,0},{2,3},{3,2},{4,5},{5,4},{6,7},{7,6},{8,9},{9,8},{10,11... | collective-permute-start | bytes 589832 | tf_op jit(solution)/shard_map/ppermute | solution.py:22
  48.8 12.7 %collective-permute-start.7 = (bf16[256,384]{1,0:T(8,128)(2,1)S(1)}, bf16[256,384]{1,0:T(8,128)(2,1)S(1)}, u32[]{:S(2)}, u32[]{:S(2)}) collective-permute-start(bf16[256,384]{1,0:T(8,128)(2,1)S(1)} %combine.4.refs_0_), channel_id=1, source_target_pairs={{0,2},{1,3},{2,0},{3,1},{4,6},{5,7},{6,4},{7,5},{8,10},{9,11},{10,... | collective-permute-start | bytes 589832 | tf_op jit(solution)/shard_map/ppermute | solution.py:22
  48.8 12.6 %collective-permute-start.14 = (bf16[2,128,1024]{2,1,0:T(8,128)(2,1)S(1)}, bf16[2,128,1024]{2,1,0:T(8,128)(2,1)S(1)}, u32[]{:S(2)}, u32[]{:S(2)}) collective-permute-start(bf16[2,128,1024]{2,1,0:T(8,128)(2,1)S(1)} %collective-permute-done.6.refs_1_.refs_17_), channel_id=1, source_target_pairs={{0,4},{4,0},{8,12},{12,8},{1,5},{5,1},{9,13},{13,9},{2,6},{6,2},{1... | collective-permute-start | bytes 1572872 | tf_op jit(solution)/shard_map/ppermute | solution.py:22
  48.9 12.6 %collective-permute-start.13 = (bf16[2,128,1024]{2,1,0:T(8,128)(2,1)S(1)}, bf16[2,128,1024]{2,1,0:T(8,128)(2,1)S(1)}, u32[]{:S(2)}, u32[]{:S(2)}) collective-permute-start(bf16[2,128,1024]{2,1,0:T(8,128)(2,1)S(1)} %copy-done), channel_id=1, source_target_pairs={{0,4},{4,0},{8,12},{12,8},{1,5},{5,1},{9,13},{13,9},{2,6},{6,2},{1... | collective-permute-start | bytes 1572872 | tf_op jit(solution)/shard_map/ppermute | solution.py:22
  54.0 10.3 %collective-permute-start.12 = (bf16[256,256]{1,0:T(8,128)(2,1)S(1)}, bf16[256,256]{1,0:T(8,128)(2,1)S(1)}, u32[]{:S(2)}, u32[]{:S(2)}) collective-permute-start(bf16[256,256]{1,0:T(8,128)(2,1)S(1)} %get-tuple-element.37), channel_id=1, source_target_pairs={{0,2},{1,3},{2,0},{3,1},{4,6},{5,7},{6,4},{7,5},{8,10},{9,11},{10,... | collective-permute-start | bytes 393224 | tf_op jit(solution)/shard_map/ppermute | solution.py:22

commit v3 on v2

--- a/solution.py
+++ b/solution.py
@@ -14,6 +14,7 @@
 bf16 = jnp.bfloat16
 hint = pl.CostEstimate(flops=1, bytes_accessed=1, transcendentals=0)
 long = pl.CostEstimate(flops=10**11, bytes_accessed=10**9, transcendentals=0)
+short = pl.CostEstimate(flops=10**9, bytes_accessed=10**6, transcendentals=0)
 mid = pl.CostEstimate(flops=8 * 10**9, bytes_accessed=8 * 10**6, transcendentals=0)
 
 
@@ -369,82 +370,108 @@
     )(*waits, *arrays)
 
 
-def finish_kernel(*refs, offsets, widths, first, n_rep, per_block, held):
+def pick_kernel(*refs, n_rep, per_block, held):
     table, refs = (*refs[:4], held), refs[4:]
-    addends = []
-    for part_offsets in offsets:
-        addends.append(list(zip(refs, part_offsets)))
-        refs = refs[len(part_offsets) :]
-    low_ref, got_ref, refs = refs[0], refs[1], refs[2:]
-    ups, refs = refs[:n_rep], refs[n_rep:]
-    out_ref, delta_ref, done_ref, sem = refs[-4:]
-    steps = out_ref.shape[1]
-    total_rows, rank_most = low_ref.shape
-    low = low_ref[...] + got_ref[:, got_ref.shape[1] - rank_most :].astype(f32)
-    column = lax.broadcasted_iota(jnp.int32, (per_block, rank_most), 1)
-    here_columns = slice(first, first + sum(widths))
-    for start in range(0, total_rows, per_block):
-        home, place, rank = block_place(table, start // per_block)
-        here = slice(start, start + per_block)
+    ups, (up_ref, scale_ref) = refs[:n_rep], refs[n_rep:]
+    column = lax.broadcasted_iota(jnp.int32, (per_block, scale_ref.shape[1]), 1)
+    for b in range(up_ref.shape[0]):
+        home, place, rank = block_place(table, b)
         factor = adapter_alpha / rank.astype(f32)
-        scaled = jnp.where(column < rank, low[here] * factor, 0.0).astype(bf16)
+        scale_ref[b * per_block : (b + 1) * per_block, :] = jnp.where(column < rank, factor, 0.0)
         for i in range(n_rep):
 
             @pl.when(home == i)
             def _():
-                delta_ref[here, :] = jnp.dot(
-                    scaled, ups[i][place, :, here_columns], preferred_element_type=f32
-                )
-
-    for start in range(0, total_rows, per_block):
-        here = slice(start, start + per_block)
-        at = 0
-        for pairs, width in zip(addends, widths):
-            there = slice(at, at + width)
-            total = sum(a[here, off : off + width].astype(f32) for a, off in pairs)
-            total += delta_ref[here, there].astype(bf16).astype(f32)
-            for r in range(per_block // steps):
-                done_ref[start // steps + r, :, there] = total[r * steps : (r + 1) * steps].astype(bf16)
-            at += width
-    copy = pltpu.make_async_copy(done_ref, out_ref.at[:, :, here_columns], sem)
-    copy.start()
-    copy.wait()
-
-
-def finish(finals, widths, first, low, got, ups, table, held_out, steps, columns, per_block):
-    total, rank = low.shape
-    wide = sum(widths)
-    operands = [a for addends in finals for a, _ in addends] + [low, got, *ups]
-    in_specs = [pl.BlockSpec(memory_space=pltpu.SMEM)] * len(table)
-    in_specs += [pl.BlockSpec(memory_space=pltpu.VMEM)] * len(operands)
-    aliases = {}
-    if held_out is not None:
-        aliases = {len(table) + len(operands): 0}
-        operands.append(held_out)
-        in_specs.append(pl.BlockSpec(memory_space=pl.ANY))
-    return pl.pallas_call(
-        functools.partial(
-            finish_kernel,
-            offsets=[[off for _, off in addends] for addends in finals],
-            widths=widths,
-            first=first,
-            n_rep=len(ups),
-            per_block=per_block,
-            held=ups[0].shape[0],
-        ),
-        in_specs=in_specs,
-        out_specs=pl.BlockSpec(memory_space=pl.ANY),
-        out_shape=jax.ShapeDtypeStruct((total // steps, steps, columns), bf16),
-        scratch_shapes=[
-            pltpu.VMEM((total, wide), f32),
-            pltpu.VMEM((total // steps, steps, wide), bf16),
-            pltpu.SemaphoreType.DMA,
+                up_ref[b] = ups[i][place]
+
+
+def pick(ups, table, blocks, per_block):
+    held, rank, columns = ups[0].shape
+    vmem = pl.BlockSpec(memory_space=pltpu.VMEM)
+    return pl.pallas_call(
+        functools.partial(pick_kernel, n_rep=len(ups), per_block=per_block, held=held),
+        in_specs=[pl.BlockSpec(memory_space=pltpu.SMEM)] * len(table) + [vmem] * len(ups),
+        out_specs=[vmem] * 2,
+        out_shape=[
+            jax.ShapeDtypeStruct((blocks, rank, columns), bf16),
+            jax.ShapeDtypeStruct((blocks * per_block, rank), f32),
         ],
-        input_output_aliases=aliases,
         compiler_params=pltpu.CompilerParams(vmem_limit_bytes=12 << 20),
         cost_estimate=hint,
+        name="pick",
+    )(*map(in_hbm, table), *ups)
+
+
+def add_up_kernel(*refs, offsets, widths):
+    *refs, _, out_ref = refs
+    at = 0
+    for part_offsets, width in zip(offsets, widths):
+        addends, refs = refs[: len(part_offsets)], refs[len(part_offsets) :]
+        total = sum(a[:, off : off + width].astype(f32) for a, off in zip(addends, part_offsets))
+        out_ref[:, at : at + width] = total
+        at += width
+
+
+def add_up(finals, widths, wait):
+    arrays = [a for addends in finals for a, _ in addends]
+    vmem = pl.BlockSpec(memory_space=pltpu.VMEM)
+    return pl.pallas_call(
+        functools.partial(
+            add_up_kernel, offsets=[[off for _, off in addends] for addends in finals], widths=widths
+        ),
+        in_specs=[vmem] * len(arrays) + [pl.BlockSpec(memory_space=pl.ANY)],
+        out_specs=vmem,
+        out_shape=jax.ShapeDtypeStruct((arrays[0].shape[0], sum(widths)), f32),
+        compiler_params=pltpu.CompilerParams(vmem_limit_bytes=12 << 20),
+        cost_estimate=long,
+        name="add_up",
+    )(*arrays, wait)
+
+
+def finish_kernel(base_ref, low_ref, got_ref, up_ref, scale_ref, *refs, offsets, per_block):
+    *addends, out_ref, done_ref, sems = refs
+    reqs, steps, columns = done_ref.shape
+    blocks, rank, _ = up_ref.shape
+    first = base_ref.shape[1]
+    low = low_ref[...] + got_ref[:, got_ref.shape[1] - rank :].astype(f32)
+    scaled = (low * scale_ref[...]).astype(bf16)
+    deltas = [
+        jnp.dot(scaled[b * per_block : (b + 1) * per_block], up_ref[b], preferred_element_type=f32)
+        for b in range(blocks)
+    ]
+    copies = []
+    for b in range(blocks):
+        here = slice(b * per_block, (b + 1) * per_block)
+        delta = deltas[b].astype(bf16).astype(f32)
+        last = sum(a[here, off : off + columns - first].astype(f32) for a, off in zip(addends, offsets))
+        for there, total in (
+            (slice(0, first), base_ref[here, :] + delta[:, :first]),
+            (slice(first, columns), last + delta[:, first:]),
+        ):
+            for r in range(per_block // steps):
+                at = b * per_block // steps + r
+                done_ref[at, :, there] = total[r * steps : (r + 1) * steps].astype(bf16)
+        mine = pl.ds(b * reqs // blocks, reqs // blocks)
+        copies.append(pltpu.make_async_copy(done_ref.at[mine], out_ref.at[mine], sems.at[b]))
+        copies[-1].start()
+    for copy in copies:
+        copy.wait()
+
+
+def finish(base, addends, low, got, up, scale, steps, columns, per_block):
+    total = low.shape[0]
+    shape = (total // steps, steps, columns)
+    arrays = [base, low, got, up, scale, *(a for a, _ in addends)]
+    return pl.pallas_call(
+        functools.partial(finish_kernel, offsets=[off for _, off in addends], per_block=per_block),
+        in_specs=[pl.BlockSpec(memory_space=pltpu.VMEM)] * len(arrays),
+        out_specs=pl.BlockSpec(memory_space=pl.ANY),
+        out_shape=jax.ShapeDtypeStruct(shape, bf16),
+        scratch_shapes=[pltpu.VMEM(shape, bf16), pltpu.SemaphoreType.DMA((up.shape[0],))],
+        compiler_params=pltpu.CompilerParams(vmem_limit_bytes=16 << 20),
+        cost_estimate=hint,
         name="finish",
-    )(*map(in_hbm, table), *operands)
+    )(*arrays)
 
 
 def halving_order(n):
@@ -527,13 +554,13 @@
         while bit < n_tp:
             wide //= 2
             first = bit == 2
-            waits = last + ([up_across] if q == 1 else []) + ([finals[q - 2][-1][0]] if q >= 2 else [])
+            waits = last + []
             out = combine(
                 addends,
                 wide,
                 low if q == parts - 1 else None,
                 waits if first else [],
-                (long if q else mid) if first else hint,
+                (mid, long, short)[q] if first else hint,
             )
             if first:
                 last = [out[0]]
@@ -557,9 +584,11 @@
                 last,
             )
             gots.append(swap(send, "tp", 1))
-        if q == 1:
+        if q == 0:
             ups = relay(adapter_up_weight, up_across, last[0])
-    return finish(finals, widths, 0, low, got, ups, table, None, steps, columns, per_block)
+    up, scale = pick(ups, table, blocks, per_block)
+    base = add_up(finals[:-1], widths[:-1], up)
+    return finish(base, finals[-1], low, got, up, scale, steps, columns, per_block)
 
 
 def solution(mesh):

time: 67.3 us -> 65.6 us (0.975)
  starting transfers between devices: 15.6 us -> 14.6 us
    ppermute x15, starting transfers between devices: 15.6 us -> 14.6 us  [swap(): return lax.ppermute(x, axis, [(i, i ^ bit) for i in range(n)])]
    pallas_call x1 -> x3, Pallas kernels: 2.75 us -> 2.2 us  [the longest x1 1.04 us: finish(): pl.pallas_call(functools.partial(finish_kernel, offsets=[off for _, off i...]
  transfers between devices with their start and end apart: 15 -> 15, of which waited for: 8 -> 8; matrix products, arithmetic and copies ran while one was open for 0% -> 0% of each run, Pallas kernels for 19% -> 21%
where the time goes in v3:
time: 65.6 us; the launch traced here: 65.4 us
  waiting for transfers between devices  32.5 us (50%)
  Pallas kernels  18.2 us (28%)
  starting transfers between devices  14.6 us (22%)
    ppermute x15, waiting for transfers between devices, swap(): return lax.ppermute(x, axis, [(i, i ^ bit) for i in range(n)])  32.5 us
    ppermute x15, starting transfers between devices, swap(): return lax.ppermute(x, axis, [(i, i ^ bit) for i in range(n)])  14.6 us
    pallas_call x2, Pallas kernels, attend(): pl.pallas_call(functools.partial(attend_kernel, pieces=pieces, n_tp=n_tp,...  6.94 us
    pallas_call x1, Pallas kernels, project_rest(): pl.pallas_call(functools.partial(project_rest_kernel, order=order, widths...  4.02 us
    pallas_call x1, Pallas kernels, project_last(): pl.pallas_call(functools.partial(project_last_kernel, owners=owners, widt...  2.57 us
    pallas_call x1, Pallas kernels, load(): pl.pallas_call(functools.partial(load_kernel, owners=owners, part=part, c...  1.56 us
  transfers between devices with their start and end apart: 15, of which 8 were waited for; matrix products, arithmetic and copies ran while one was open for 0% of the time, Pallas kernels for 21%

profile of v3, /device:TPU:0, one launch (start us, length us, event | category | flops | bytes accessed | tf_op | source)
XLA Modules:
  0.0 65.4 jit_solution(636175005367921421)
XLA Ops:
  0.0 3.5 %attention.2 = (bf16[64,1024]{1,0:T(8,128)(2,1)S(1)}, bf16[64,1024]{1,0:T(8,128)(2,1)S(1)}) custom-call(s32[1]{0:T(128)} %bitcast.me_ref, s32[16]{0:T(128)} %len_ref.3, bf16[16,4,4096]{2,1,0:T(4,128)(2,1)} %q_ref.3, bf16[16,4,4,128]{3,2,1,0:T(4,128)(2,1)} %dk_ref.3, bf16[16,4,4,128]{3,2,1,0:T(4,128)(2,1)} %dv_ref.3, bf16[16,4,128,128]{3,2,1,0:T(8,128)(2,1)} %refs_1_.5, ...), custom_call_target="tpu_custom_call" | custom-call | flops 1 | bytes 1 | tf_op jit(solution)/shard_map/attention/pallas_call | solution.py:125
  3.5 5.1 %collective-permute-start.2 = (bf16[64,1024]{1,0:T(8,128)(2,1)S(1)}, bf16[64,1024]{1,0:T(8,128)(2,1)S(1)}, u32[]{:S(2)}, u32[]{:S(2)}) collective-permute-start(bf16[64,1024]{1,0:T(8,128)(2,1)S(1)} %get-tuple-element.25.refs_4_), channel_id=1, source_target_pairs={{0,3},{1,2},{2,1},{3,0},{4,7},{5,6},{6,5},{7,4},{8,11},{9,10},{10,... | collective-permute-start | bytes 393224 | tf_op jit(solution)/shard_map/ppermute | solution.py:23
  8.6 3.5 %attention.3 = (bf16[64,1024]{1,0:T(8,128)(2,1)S(1)}, bf16[64,1024]{1,0:T(8,128)(2,1)S(1)}) custom-call(s32[1]{0:T(128)} %bitcast.me_ref, s32[16]{0:T(128)} %len_ref.3, bf16[16,4,4096]{2,1,0:T(4,128)(2,1)} %q_ref.3, bf16[16,4,4,128]{3,2,1,0:T(4,128)(2,1)} %dk_ref.3, bf16[16,4,4,128]{3,2,1,0:T(4,128)(2,1)} %dv_ref.3, bf16[16,4,128,128]{3,2,1,0:T(8,128)(2,1)} %refs_1_.5, ...), custom_call_target="tpu_custom_call" | custom-call | flops 1 | bytes 1 | tf_op jit(solution)/shard_map/attention/pallas_call | solution.py:125
  12.1 0.7 %collective-permute-start = (bf16[64,1024]{1,0:T(8,128)(2,1)S(1)}, bf16[64,1024]{1,0:T(8,128)(2,1)S(1)}, u32[]{:S(2)}, u32[]{:S(2)}) collective-permute-start(bf16[64,1024]{1,0:T(8,128)(2,1)S(1)} %get-tuple-element.26), channel_id=1, source_target_pairs={{0,1},{1,0},{2,3},{3,2},{4,5},{5,4},{6,7},{7,6},{8,9},{9,8},{10,11... | collective-permute-start | bytes 393224 | tf_op jit(solution)/shard_map/ppermute | solution.py:23
  12.8 1.6 %load.1.w_ref = bf16[1024,1024]{1,0:T(8,128)(2,1)S(1)} custom-call(s32[1]{0:T(128)} %bitcast.me_ref, bf16[1024,4096]{1,0:T(8,128)(2,1)} %refs_5_.1, bf16[64,1024]{1,0:T(8,128)(2,1)S(1)} %get-tuple-element.27.refs_0_), custom_call_target="tpu_custom_call" | custom-call | flops 1 | bytes 1 | tf_op jit(solution)/shard_map/load/pallas_call | solution.py:168
  14.3 1.7 %collective-permute-start.11 = (bf16[2,1024,128]{2,1,0:T(8,128)(2,1)}, bf16[2,1024,128]{2,1,0:T(8,128)(2,1)}, u32[]{:S(2)}, u32[]{:S(2)}) collective-permute-start(bf16[2,1024,128]{2,1,0:T(8,128)(2,1)} %refs_6_), channel_id=1, source_target_pairs={{0,8},{4,12},{8,0},{12,4},{1,9},{5,13},{9,1},{13,5},{2,10},{6,14},... | collective-permute-start | bytes 1572872 | tf_op jit(solution)/shard_map/ppermute | solution.py:23
  16.1 3.7 %collective-permute-done.1.refs_1_ = bf16[64,1024]{1,0:T(8,128)(2,1)S(1)} collective-permute-done((bf16[64,1024]{1,0:T(8,128)(2,1)S(1)}, bf16[64,1024]{1,0:T(8,128)(2,1)S(1)}, u32[]{:S(2)}, u32[]{:S(2)}) %collective-permute-start.1) | collective-permute-done | bytes 131104 | tf_op jit(solution)/shard_map/ppermute | solution.py:23
  19.9 0.7 %projection.1 = (bf16[256,1024]{1,0:T(8,128)(2,1)S(1)}, bf16[256,1024]{1,0:T(8,128)(2,1)S(1)}) custom-call(s32[1]{0:T(128)} %bitcast.me_ref, bf16[64,1024]{1,0:T(8,128)(2,1)S(1)} %collective-permute-done.piece_ref, bf16[1024,1024]{1,0:T(8,128)(2,1)S(1)} %load.1.w_ref, bf16[256,1024]{1,0:T(8,128)(2,1)S(1)} %gather.1._), custom_call_target="tpu_custom_call", output_to_operand_aliasing={{1}: (3, {})} | custom-call | flops 99999997952 | bytes 1000000000 | tf_op jit(solution)/shard_map/projection/pallas_call | solution.py:218
  20.7 4.0 %projection_rest.1 = (bf16[256,768]{1,0:T(8,128)(2,1)S(1)}, bf16[256,2048]{1,0:T(8,128)(2,1)S(1)}) custom-call(s32[1]{0:T(128)} %bitcast.me_ref, bf16[256,1024]{1,0:T(8,128)(2,1)S(1)} %get-tuple-element.29.x_ref.refs_4_, bf16[1024,4096]{1,0:T(8,128)(2,1)} %refs_5_.1), custom_call_target="tpu_custom_call" | custom-call | flops 1 | bytes 1 | tf_op jit(solution)/shard_map/projection_rest/pallas_call | solution.py:260
  24.8 2.1 %collective-permute-start.5 = (bf16[256,768]{1,0:T(8,128)(2,1)S(1)}, bf16[256,768]{1,0:T(8,128)(2,1)S(1)}, u32[]{:S(2)}, u32[]{:S(2)}) collective-permute-start(bf16[256,768]{1,0:T(8,128)(2,1)S(1)} %get-tuple-element.32), channel_id=1, source_target_pairs={{0,1},{1,0},{2,3},{3,2},{4,5},{5,4},{6,7},{7,6},{8,9},{9,8},{10,11... | collective-permute-start | bytes 1179656 | tf_op jit(solution)/shard_map/ppermute | solution.py:23
  26.9 1.5 %collective-permute-start.8 = (bf16[2,128,1024]{2,1,0:T(8,128)(2,1)S(1)}, bf16[2,128,1024]{2,1,0:T(8,128)(2,1)S(1)}, u32[]{:S(2)}, u32[]{:S(2)}) collective-permute-start(bf16[2,128,1024]{2,1,0:T(8,128)(2,1)S(1)} %copy-done), channel_id=1, source_target_pairs={{0,8},{4,12},{8,0},{12,4},{1,9},{5,13},{9,1},{13,5},{2,10},{6,14},... | collective-permute-start | bytes 1572872 | tf_op jit(solution)/shard_map/ppermute | solution.py:23
  28.4 10.0 %collective-permute-done.3.refs_1_ = bf16[256,1024]{1,0:T(8,128)(2,1)S(1)} collective-permute-done((bf16[256,1024]{1,0:T(8,128)(2,1)S(1)}, bf16[256,1024]{1,0:T(8,128)(2,1)S(1)}, u32[]{:S(2)}, u32[]{:S(2)}) %collective-permute-start.3) | collective-permute-done | bytes 524320 | tf_op jit(solution)/shard_map/ppermute | solution.py:23
  38.8 2.1 %collective-permute-done.8.refs_6_ = bf16[2,128,1024]{2,1,0:T(8,128)(2,1)S(1)} collective-permute-done((bf16[2,128,1024]{2,1,0:T(8,128)(2,1)S(1)}, bf16[2,128,1024]{2,1,0:T(8,128)(2,1)S(1)}, u32[]{:S(2)}, u32[]{:S(2)}) %collective-permute-start.8) | collective-permute-done | bytes 524320 | tf_op jit(solution)/shard_map/ppermute | solution.py:23
  40.9 0.5 collective-permute-start.7
  41.4 2.6 %projection_last.1 = (bf16[256,384]{1,0:T(8,128)(2,1)S(1)}, f32[256,128]{1,0:T(8,128)S(1)}) custom-call(s32[1]{0:T(128)} %bitcast.me_ref, s32[1]{0:T(128)} %bitcast.1.refs_0_, s32[4]{0:T(128)} %refs_1_.7, s32[8]{0:T(128)} %refs_2_.7, s32[8]{0:T(128)} %refs_3_.7, bf16[256,1024]{1,0:T(8,128)(2,1)S(1)} %get-tuple-element.29.x_ref.refs_4_, ...), custom_call_target="tpu_custom_call" | custom-call | flops 1 | bytes 1 | tf_op jit(solution)/shard_map/projection_last/pallas_call | solution.py:302
  44.0 0.6 collective-permute-start.13
  44.6 0.9 %collective-permute-done.5.refs_2_.refs_4_ = bf16[256,768]{1,0:T(8,128)(2,1)S(1)} collective-permute-done((bf16[256,768]{1,0:T(8,128)(2,1)S(1)}, bf16[256,768]{1,0:T(8,128)(2,1)S(1)}, u32[]{:S(2)}, u32[]{:S(2)}) %collective-permute-start.5) | collective-permute-done | bytes 393248 | tf_op jit(solution)/shard_map/ppermute | solution.py:23
  45.5 1.5 %collective-permute-start.6 = (bf16[256,384]{1,0:T(8,128)(2,1)S(1)}, bf16[256,384]{1,0:T(8,128)(2,1)S(1)}, u32[]{:S(2)}, u32[]{:S(2)}) collective-permute-start(bf16[256,384]{1,0:T(8,128)(2,1)S(1)} %combine.4.refs_0_), channel_id=1, source_target_pairs={{0,2},{1,3},{2,0},{3,1},{4,6},{5,7},{6,4},{7,5},{8,10},{9,11},{10,... | collective-permute-start | bytes 589832 | tf_op jit(solution)/shard_map/ppermute | solution.py:23
  47.1 1.0 %pick.1 = (bf16[4,128,1024]{2,1,0:T(8,128)(2,1)S(1)}, f32[256,128]{1,0:T(8,128)S(1)}) custom-call(s32[1]{0:T(128)} %bitcast.1.refs_0_, s32[4]{0:T(128)} %refs_1_.7, s32[8]{0:T(128)} %refs_2_.7, s32[8]{0:T(128)} %refs_3_.7, bf16[2,128,1024]{2,1,0:T(8,128)(2,1)S(1)} %copy-done, bf16[2,128,1024]{2,1,0:T(8,128)(2,1)S(1)} %collective-permute-done.7.refs_5_, ...), custom_call_target="tpu_custom_call" | custom-call | flops 1 | bytes 1 | tf_op jit(solution)/shard_map/pick/pallas_call | solution.py:391
  48.1 7.0 %collective-permute-done.13.refs_2_.refs_1_ = bf16[256,384]{1,0:T(8,128)(2,1)S(1)} collective-permute-done((bf16[256,384]{1,0:T(8,128)(2,1)S(1)}, bf16[256,384]{1,0:T(8,128)(2,1)S(1)}, u32[]{:S(2)}, u32[]{:S(2)}) %collective-permute-start.13) | collective-permute-done | bytes 196640 | tf_op jit(solution)/shard_map/ppermute | solution.py:23
  55.1 0.5 collective-permute-start.14
  55.6 6.6 %collective-permute-done.6.refs_5_ = bf16[256,384]{1,0:T(8,128)(2,1)S(1)} collective-permute-done((bf16[256,384]{1,0:T(8,128)(2,1)S(1)}, bf16[256,384]{1,0:T(8,128)(2,1)S(1)}, u32[]{:S(2)}, u32[]{:S(2)}) %collective-permute-start.6) | collective-permute-done | bytes 196640 | tf_op jit(solution)/shard_map/ppermute | solution.py:23
  62.4 2.0 %collective-permute-done.14.got_ref.refs_2_ = bf16[256,256]{1,0:T(8,128)(2,1)S(1)} collective-permute-done((bf16[256,256]{1,0:T(8,128)(2,1)S(1)}, bf16[256,256]{1,0:T(8,128)(2,1)S(1)}, u32[]{:S(2)}, u32[]{:S(2)}) %collective-permute-start.14) | collective-permute-done | bytes 131104 | tf_op jit(solution)/shard_map/ppermute | solution.py:23
  64.3 1.0 %finish.1 = bf16[64,4,1024]{2,1,0:T(4,128)(2,1)} custom-call(f32[256,896]{1,0:T(8,128)S(1)} %add_up.1.base_ref, f32[256,128]{1,0:T(8,128)S(1)} %get-tuple-element.42.low_ref, bf16[256,256]{1,0:T(8,128)(2,1)S(1)} %collective-permute-done.14.got_ref.refs_2_, bf16[4,128,1024]{2,1,0:T(8,128)(2,1)S(1)} %get-tuple-element.36.refs_6_.up_ref, ...), custom_call_target="tpu_custom_call" | custom-call | flops 1 | bytes 1 | tf_op jit(solution)/shard_map/finish/pallas_call | solution.py:465
  (21 shorter events, 0.9 us)
Async XLA Ops:
  3.5 12.6 %collective-permute-start.2 = (bf16[64,1024]{1,0:T(8,128)(2,1)S(1)}, bf16[64,1024]{1,0:T(8,128)(2,1)S(1)}, u32[]{:S(2)}, u32[]{:S(2)}) collective-permute-start(bf16[64,1024]{1,0:T(8,128)(2,1)S(1)} %get-tuple-element.25.refs_4_), channel_id=1, source_target_pairs={{0,3},{1,2},{2,1},{3,0},{4,7},{5,6},{6,5},{7,4},{8,11},{9,10},{10,... | collective-permute-start | bytes 393224 | tf_op jit(solution)/shard_map/ppermute | solution.py:23
  8.6 11.2 %collective-permute-start.1 = (bf16[64,1024]{1,0:T(8,128)(2,1)S(1)}, bf16[64,1024]{1,0:T(8,128)(2,1)S(1)}, u32[]{:S(2)}, u32[]{:S(2)}) collective-permute-start(bf16[64,1024]{1,0:T(8,128)(2,1)S(1)} %get-tuple-element.28), channel_id=1, source_target_pairs={{0,2},{1,3},{2,0},{3,1},{4,6},{5,7},{6,4},{7,5},{8,10},{9,11},{10,... | collective-permute-start | bytes 393224 | tf_op jit(solution)/shard_map/ppermute | solution.py:23
  12.1 7.8 %collective-permute-start = (bf16[64,1024]{1,0:T(8,128)(2,1)S(1)}, bf16[64,1024]{1,0:T(8,128)(2,1)S(1)}, u32[]{:S(2)}, u32[]{:S(2)}) collective-permute-start(bf16[64,1024]{1,0:T(8,128)(2,1)S(1)} %get-tuple-element.26), channel_id=1, source_target_pairs={{0,1},{1,0},{2,3},{3,2},{4,5},{5,4},{6,7},{7,6},{8,9},{9,8},{10,11... | collective-permute-start | bytes 393224 | tf_op jit(solution)/shard_map/ppermute | solution.py:23
  14.3 14.0 %collective-permute-start.11 = (bf16[2,1024,128]{2,1,0:T(8,128)(2,1)}, bf16[2,1024,128]{2,1,0:T(8,128)(2,1)}, u32[]{:S(2)}, u32[]{:S(2)}) collective-permute-start(bf16[2,1024,128]{2,1,0:T(8,128)(2,1)} %refs_6_), channel_id=1, source_target_pairs={{0,8},{4,12},{8,0},{12,4},{1,9},{5,13},{9,1},{13,5},{2,10},{6,14},... | collective-permute-start | bytes 1572872 | tf_op jit(solution)/shard_map/ppermute | solution.py:23
  20.6 17.7 %collective-permute-start.3 = (bf16[256,1024]{1,0:T(8,128)(2,1)S(1)}, bf16[256,1024]{1,0:T(8,128)(2,1)S(1)}, u32[]{:S(2)}, u32[]{:S(2)}) collective-permute-start(bf16[256,1024]{1,0:T(8,128)(2,1)S(1)} %get-tuple-element.31), channel_id=1, source_target_pairs={{0,1},{1,0},{2,3},{3,2},{4,5},{5,4},{6,7},{7,6},{8,9},{9,8},{10,11... | collective-permute-start | bytes 1572872 | tf_op jit(solution)/shard_map/ppermute | solution.py:23
  20.7 6.2 %copy-start = (bf16[2,128,1024]{2,1,0:T(8,128)(2,1)S(1)}, bf16[2,128,1024]{2,1,0:T(8,128)(2,1)}, u32[]{:S(2)}) copy-start(bf16[2,128,1024]{2,1,0:T(8,128)(2,1)} %refs_4_) | copy-start | bytes 1572868
  24.8 16.1 %collective-permute-start.10 = (bf16[2,1024,128]{2,1,0:T(8,128)(2,1)}, bf16[2,1024,128]{2,1,0:T(8,128)(2,1)S(1)}, u32[]{:S(2)}, u32[]{:S(2)}) collective-permute-start(bf16[2,1024,128]{2,1,0:T(8,128)(2,1)} %refs_6_), channel_id=1, source_target_pairs={{0,4},{4,0},{8,12},{12,8},{1,5},{5,1},{9,13},{13,9},{2,6},{6,2},{1... | collective-permute-start | bytes 1572872 | tf_op jit(solution)/shard_map/ppermute | solution.py:23
  24.8 20.6 %collective-permute-start.5 = (bf16[256,768]{1,0:T(8,128)(2,1)S(1)}, bf16[256,768]{1,0:T(8,128)(2,1)S(1)}, u32[]{:S(2)}, u32[]{:S(2)}) collective-permute-start(bf16[256,768]{1,0:T(8,128)(2,1)S(1)} %get-tuple-element.32), channel_id=1, source_target_pairs={{0,1},{1,0},{2,3},{3,2},{4,5},{5,4},{6,7},{7,6},{8,9},{9,8},{10,11... | collective-permute-start | bytes 1179656 | tf_op jit(solution)/shard_map/ppermute | solution.py:23
  26.9 14.0 %collective-permute-start.8 = (bf16[2,128,1024]{2,1,0:T(8,128)(2,1)S(1)}, bf16[2,128,1024]{2,1,0:T(8,128)(2,1)S(1)}, u32[]{:S(2)}, u32[]{:S(2)}) collective-permute-start(bf16[2,128,1024]{2,1,0:T(8,128)(2,1)S(1)} %copy-done), channel_id=1, source_target_pairs={{0,8},{4,12},{8,0},{12,4},{1,9},{5,13},{9,1},{13,5},{2,10},{6,14},... | collective-permute-start | bytes 1572872 | tf_op jit(solution)/shard_map/ppermute | solution.py:23
  28.4 13.0 %collective-permute-start.12 = (bf16[2,1024,128]{2,1,0:T(8,128)(2,1)}, bf16[2,1024,128]{2,1,0:T(8,128)(2,1)S(1)}, u32[]{:S(2)}, u32[]{:S(2)}) collective-permute-start(bf16[2,1024,128]{2,1,0:T(8,128)(2,1)} %collective-permute-done.11.refs_8_), channel_id=1, source_target_pairs={{0,4},{4,0},{8,12},{12,8},{1,5},{5,1},{9,13},{13,9},{2,6},{6,2},{1... | collective-permute-start | bytes 1572872 | tf_op jit(solution)/shard_map/ppermute | solution.py:23
  38.4 23.8 %collective-permute-start.4 = (bf16[256,512]{1,0:T(8,128)(2,1)S(1)}, bf16[256,512]{1,0:T(8,128)(2,1)S(1)}, u32[]{:S(2)}, u32[]{:S(2)}) collective-permute-start(bf16[256,512]{1,0:T(8,128)(2,1)S(1)} %combine.3.refs_0_.refs_10_), channel_id=1, source_target_pairs={{0,2},{1,3},{2,0},{3,1},{4,6},{5,7},{6,4},{7,5},{8,10},{9,11},{10,... | collective-permute-start | bytes 786440 | tf_op jit(solution)/shard_map/ppermute | solution.py:23
  40.9 6.2 %collective-permute-start.9 = (bf16[2,128,1024]{2,1,0:T(8,128)(2,1)S(1)}, bf16[2,128,1024]{2,1,0:T(8,128)(2,1)S(1)}, u32[]{:S(2)}, u32[]{:S(2)}) collective-permute-start(bf16[2,128,1024]{2,1,0:T(8,128)(2,1)S(1)} %collective-permute-done.8.refs_6_), channel_id=1, source_target_pairs={{0,4},{4,0},{8,12},{12,8},{1,5},{5,1},{9,13},{13,9},{2,6},{6,2},{1... | collective-permute-start | bytes 1572872 | tf_op jit(solution)/shard_map/ppermute | solution.py:23
  40.9 6.2 %collective-permute-start.7 = (bf16[2,128,1024]{2,1,0:T(8,128)(2,1)S(1)}, bf16[2,128,1024]{2,1,0:T(8,128)(2,1)S(1)}, u32[]{:S(2)}, u32[]{:S(2)}) collective-permute-start(bf16[2,128,1024]{2,1,0:T(8,128)(2,1)S(1)} %copy-done), channel_id=1, source_target_pairs={{0,4},{4,0},{8,12},{12,8},{1,5},{5,1},{9,13},{13,9},{2,6},{6,2},{1... | collective-permute-start | bytes 1572872 | tf_op jit(solution)/shard_map/ppermute | solution.py:23
  44.0 11.1 %collective-permute-start.13 = (bf16[256,384]{1,0:T(8,128)(2,1)S(1)}, bf16[256,384]{1,0:T(8,128)(2,1)S(1)}, u32[]{:S(2)}, u32[]{:S(2)}) collective-permute-start(bf16[256,384]{1,0:T(8,128)(2,1)S(1)} %get-tuple-element.40), channel_id=1, source_target_pairs={{0,1},{1,0},{2,3},{3,2},{4,5},{5,4},{6,7},{7,6},{8,9},{9,8},{10,11... | collective-permute-start | bytes 589832 | tf_op jit(solution)/shard_map/ppermute | solution.py:23
  45.5 16.7 %collective-permute-start.6 = (bf16[256,384]{1,0:T(8,128)(2,1)S(1)}, bf16[256,384]{1,0:T(8,128)(2,1)S(1)}, u32[]{:S(2)}, u32[]{:S(2)}) collective-permute-start(bf16[256,384]{1,0:T(8,128)(2,1)S(1)} %combine.4.refs_0_), channel_id=1, source_target_pairs={{0,2},{1,3},{2,0},{3,1},{4,6},{5,7},{6,4},{7,5},{8,10},{9,11},{10,... | collective-permute-start | bytes 589832 | tf_op jit(solution)/shard_map/ppermute | solution.py:23
  55.1 9.2 %collective-permute-start.14 = (bf16[256,256]{1,0:T(8,128)(2,1)S(1)}, bf16[256,256]{1,0:T(8,128)(2,1)S(1)}, u32[]{:S(2)}, u32[]{:S(2)}) collective-permute-start(bf16[256,256]{1,0:T(8,128)(2,1)S(1)} %get-tuple-element.43), channel_id=1, source_target_pairs={{0,2},{1,3},{2,0},{3,1},{4,6},{5,7},{6,4},{7,5},{8,10},{9,11},{10,... | collective-permute-start | bytes 393224 | tf_op jit(solution)/shard_map/ppermute | solution.py:23
